TPU v7x, 128 devices: a whole 4x4x4 slice. The times are simulated.
128 devices in a mesh: ctx: 16 (over x_lo, z, core), head: 8 (over x_hi, y).
Axes of the slice: x: 4 (x_hi: 2, x_lo: 2; x = x_hi * 2 + x_lo), y: 4, z: 4, core: 2. Of those that a mesh axis runs over, the one named last changes fastest.
Arguments:
- queries: bfloat16 [1024, 8192], P('ctx', 'head'), may hold values from -40 to 40
- stretch_keys: bfloat16 [1024, 1024], P('ctx', 'head'), may hold values from -4 to 4
- stretch_values: bfloat16 [1024, 1024], P('ctx', 'head'), may hold values from -5 to 5
- cache_keys: bfloat16 [32768, 1024], P('ctx', 'head'), may hold values from -4 to 4
- cache_values: bfloat16 [32768, 1024], P('ctx', 'head'), may hold values from -5 to 5
- head_types: int32 [8], replicated, may hold values from 0 to 1, as said below
- sink_blocks: int32 [8], replicated, may hold values from 1 to 4, as said below
- window_blocks: int32 [8], replicated, may hold values from 1 to 8, as said below
Outputs:
- attended: bfloat16 [1024, 8192], P('ctx', 'head')
Inputs may be any that keep to these rules, and one draw needn't show every extreme that they name: `head_types`: exactly half of the 8 heads are retrieval heads. `sink_blocks`: some head has 4. `window_blocks`: some head has 8.
All inputs are finite; a program needn't handle non-finite values.
Results may differ from a plain program's by a relative error of at most 0.0044.
Values may be sent and summed in bfloat16 or wider, within the bound.
No kernel may reach another device: no remote copies, remote signals or barrier semaphores. Data moves between devices by JAX's collectives and lax.ppermute only.
A program may use at most 64 MiB of HBM per device.

v0:
```python
import functools
import math

import jax
import jax.numpy as jnp
from jax import lax
from jax.experimental import pallas as pl
from jax.experimental.pallas import tpu as pltpu
from jax.sharding import PartitionSpec as P

D = 128
BLOCK = 128
SCALE = math.log2(math.e) / math.sqrt(D)
NEG = -1e30
HEADROOM = 40.0
SAFE = 2.0**100
SAMPLE = 256
CUT = 1536
SEGMENT = 512
UNROLL = False
VMEM_LIMIT = 32 * 2**20
NT = (((1,), (1,)), ((), ()))
F32 = jnp.float32
BF16 = jnp.bfloat16


def scores_of(query, keys):
    return lax.dot_general(query, keys, NT, preferred_element_type=F32)


def row_max(x):
    peak = functools.reduce(
        jnp.maximum, [x[:, i : i + D] for i in range(0, x.shape[1], D)]
    )
    return jnp.broadcast_to(jnp.max(peak, axis=1, keepdims=True), (x.shape[0], D))


def attend_kernel(geom, *refs):
    steps, sources, shard, ctx_count, state_in, emit = geom
    n, n_src = len(steps), len(sources)
    kinds, sinks, windows = refs[:3]
    q_in = refs[3 : 3 + n]
    kv = refs[3 + n : 3 + n + n_src]
    rest = refs[3 + n + n_src :]
    if state_in:
        old, rest = rest[0], rest[1:]
    out, q_buf = rest[0], rest[1]
    state = rest[2] if emit else out
    group = q_in[0].shape[1] // D
    tokens = q_in[0].shape[0]
    q_rows = group * tokens
    ctx = lax.axis_index("ctx")
    head = lax.axis_index("head")
    kind = kinds[head]
    sink = sinks[head]
    window = windows[head]
    total_blocks = ctx_count * shard // BLOCK

    for c in range(n):
        for g in range(group):
            q_buf[c, g * tokens : (g + 1) * tokens, :] = q_in[c][:, g * D : (g + 1) * D]
    with_stretch = [s for s in range(n_src) if sources[s][2]]
    if with_stretch:
        own = sources[with_stretch[0]][2]
        wide = len(with_stretch) * own
        column = lax.broadcasted_iota(jnp.int32, (q_rows, wide), 1)
        token = lax.broadcasted_iota(jnp.int32, (q_rows, wide), 0) % tokens
        key_pos = jnp.zeros_like(column)
        for i, s in enumerate(with_stretch):
            here = (column >= i * own) & (column < (i + 1) * own)
            key_pos = jnp.where(here, (ctx ^ sources[s][0]) * own + column - i * own, key_pos)

    def stretch_parts(c):
        keys, values = [], []
        for s in with_stretch:
            rows = sources[s][1]
            keys.append(kv[s][rows : rows + own, :])
            values.append(kv[s][2 * rows + own : 2 * rows + 2 * own, :])
        owner = jnp.int32(0)
        for i, step in enumerate(steps):
            owner = jnp.where(c == i, source_of(ctx, step), owner)
        x = scores_of(q_buf[c], jnp.concatenate(keys, 0)) * SCALE
        return x, jnp.concatenate(values, 0), key_pos <= token + owner * tokens

    def exact(c):
        if state_in:
            for i in range(3):
                state[c, i] = old[c, i]
        else:
            state[c, 0] = jnp.full((q_rows, D), NEG, F32)
            state[c, 1] = jnp.zeros((q_rows, D), F32)
            state[c, 2] = jnp.zeros((q_rows, D), F32)

        def update(x, values, mask):
            before = state[c, 0]
            if mask is not None:
                x = jnp.where(mask, x, NEG)
            now = jnp.maximum(before, row_max(x))
            fade = jnp.exp2(before - now)
            total = state[c, 1] * fade
            weights = []
            for j in range(0, x.shape[1], D):
                p = jnp.exp2(x[:, j : j + D] - now)
                if mask is not None:
                    p = jnp.where(mask[:, j : j + D], p, 0.0)
                total = total + p
                weights.append(p.astype(BF16))
            state[c, 0] = now
            state[c, 1] = total
            state[c, 2] = state[c, 2] * fade + jnp.dot(
                jnp.concatenate(weights, 1), values, preferred_element_type=F32
            )

        for s, (flip, rows, extra, first) in enumerate(sources):
            base = (ctx ^ flip) * shard + first
            low = jnp.where(kind == 1, rows, jnp.clip(sink * BLOCK - base, 0, rows))
            high = jnp.clip((total_blocks - window) * BLOCK - base, low, rows)
            span = min(SEGMENT, rows)
            low_end = (low + span - 1) // span
            skip = jnp.maximum(high // span, low_end) - low_end

            def step(j, _, s=s, v_at=rows + extra, low=low, high=high, span=span, low_end=low_end, skip=skip):
                at = pl.multiple_of(jnp.where(j < low_end, j, j + skip) * span, span)
                x = scores_of(q_buf[c], kv[s][pl.ds(at, span), :]) * SCALE
                place = at + lax.broadcasted_iota(jnp.int32, (1, span), 1)
                kept = jnp.broadcast_to((place < low) | (place >= high), x.shape)
                update(x, kv[s][pl.ds(v_at + at, span), :], kept)
                return 0

            lax.fori_loop(0, rows // span - skip, step, 0)
        if with_stretch:
            update(*stretch_parts(c))

    def fixed_stabiliser(chosen):
        segments = []
        for c in range(len(chosen)):
            for s, (_, rows, extra, _) in enumerate(sources):
                for at in range(0, rows, SEGMENT):
                    segments.append((c, s, at, rows + extra + at, min(SEGMENT, rows - at)))
            if with_stretch:
                segments.append((c, None, 0, 0, wide))
        query = [q_buf[c] for c in chosen]
        fixed, total, acc = ([None] * len(chosen) for _ in range(3))
        now = None
        for i in range(len(segments) + 1):
            later = None
            if i < len(segments):
                c, s, at, _, size = segments[i]
                if s is None:
                    later = stretch_parts(chosen[c])
                else:
                    later = (scores_of(query[c], kv[s][at : at + size, :]), None, None)
            if i > 0:
                c, s, _, at, size = segments[i - 1]
                x, values, mask = now
                if s is not None:
                    values = kv[s][at : at + size, :]
                    x = x * SCALE
                if i == 1 or segments[i - 2][0] != c:
                    if state_in:
                        fixed[c], total[c], acc[c] = (old[chosen[c], k] for k in range(3))
                    else:
                        fixed[c] = row_max(x[:, :SAMPLE]) + HEADROOM
                weights = []
                for j in range(0, size, D):
                    p = jnp.exp2(x[:, j : j + D] - fixed[c])
                    if mask is not None:
                        p = jnp.where(mask[:, j : j + D], p, 0.0)
                    total[c] = p if total[c] is None else total[c] + p
                    weights.append(p.astype(BF16))
                more = jnp.dot(jnp.concatenate(weights, 1), values, preferred_element_type=F32)
                acc[c] = more if acc[c] is None else acc[c] + more
                if i == len(segments) or segments[i][0] != c:
                    state[chosen[c], 0] = fixed[c]
                    state[chosen[c], 1] = total[c]
                    state[chosen[c], 2] = acc[c]
            now = later

    def every_exact():
        if n == 1:
            exact(0)
        else:

            def step(c, _):
                exact(c)
                return 0

            lax.fori_loop(0, n, step, 0)

    @pl.when(kind == 1)
    def _():
        if n == 1 or UNROLL:
            fixed_stabiliser(list(range(n)))
        else:

            def one(c, _):
                fixed_stabiliser([c])
                return 0

            lax.fori_loop(0, n, one, 0)
        flags = [jnp.where(state[c, 1] < SAFE, 0.0, 1.0) for c in range(n)]
        safe = jnp.max(functools.reduce(jnp.maximum, flags)) < 0.5

        @pl.when(jnp.logical_not(safe))
        def _():
            every_exact()

    @pl.when(kind != 1)
    def _():
        every_exact()

    if emit:

        def hand_out(c, _):
            total = jnp.sum(state[c, 1], axis=1, keepdims=True)
            some = total > 0.0
            total = jnp.where(some, total, 1.0)
            part = state[c, 2] / total
            out[c, :q_rows, :] = part.astype(BF16)
            log_sum = jnp.where(some, state[c, 0] + jnp.log(total) * math.log2(math.e), NEG)
            eye = lax.broadcasted_iota(jnp.int32, (D, D), 0) == lax.broadcasted_iota(
                jnp.int32, (D, D), 1
            )
            lines = []
            for i in range(0, q_rows, D):
                lines.append(
                    jnp.sum(jnp.where(eye, log_sum[i : i + D, :], 0.0), axis=0, keepdims=True)
                )
            lines = jnp.concatenate(lines, 0)
            pieces = []
            for _ in range(3):
                piece = lines.astype(BF16).astype(F32)
                pieces.append(piece)
                lines = lines - piece
            pad = 16 - 3 * (q_rows // D)
            tail = jnp.concatenate(pieces + [jnp.zeros((pad, D), F32)], 0)
            out[c, q_rows:, :] = tail.astype(BF16)
            return 0

        if n == 1:
            hand_out(0, 0)
        else:
            lax.fori_loop(0, n, hand_out, 0)


def source_of(ctx, step):
    return (ctx // 8) * 8 + (ctx % 8 - 2 * step + 8) % 8


def attend(tables, queries, steps, sources, shard, state, emit):
    n = len(steps)
    tokens, width = queries[0].shape
    q_rows = tokens * (width // D)
    geom = (
        tuple(steps),
        tuple(source[1:] for source in sources),
        shard,
        lax.axis_size("ctx"),
        state is not None,
        emit,
    )
    shape_state = (n, 3, q_rows, D)
    if emit:
        out_shape = jax.ShapeDtypeStruct((n, q_rows + 16, D), BF16)
        scratch = [pltpu.VMEM((n, q_rows, D), BF16), pltpu.VMEM(shape_state, F32)]
    else:
        out_shape = jax.ShapeDtypeStruct(shape_state, F32)
        scratch = [pltpu.VMEM((n, q_rows, D), BF16)]
    smem = pl.BlockSpec(memory_space=pltpu.SMEM)
    vmem = pl.BlockSpec(memory_space=pltpu.VMEM)
    states = [] if state is None else [state]
    pairs = n * q_rows * sum(source[2] + source[3] for source in sources)
    return pl.pallas_call(
        functools.partial(attend_kernel, geom),
        out_shape=out_shape,
        in_specs=[smem] * 3 + [vmem] * (n + len(sources) + len(states)),
        out_specs=vmem,
        scratch_shapes=scratch,
        compiler_params=pltpu.CompilerParams(vmem_limit_bytes=VMEM_LIMIT),
        cost_estimate=pl.CostEstimate(
            flops=4 * pairs * D,
            bytes_accessed=sum(4 * D * (source[2] + source[3]) for source in sources),
            transcendentals=pairs,
        ),
    )(*tables, *queries, *[source[0] for source in sources], *states)


def combine_kernel(*refs):
    *parts, out = refs
    tokens, width = out.shape
    group = width // D
    q_rows = tokens * group
    for i in range(q_rows // D):
        logs = []
        for part in parts:
            tail = part[q_rows:, :].astype(F32)
            step = q_rows // D
            logs.append(
                tail[i : i + 1] + tail[step + i : step + i + 1] + tail[2 * step + i : 2 * step + i + 1]
            )
        peak = functools.reduce(jnp.maximum, logs)
        weights = [jnp.exp2(x - peak) for x in logs]
        total = functools.reduce(jnp.add, weights)
        acc = jnp.zeros((D, D), F32)
        for part, weight in zip(parts, weights):
            spread = jnp.broadcast_to(weight / total, (D, D)).T
            acc = acc + spread * part[i * D : (i + 1) * D, :].astype(F32)
        for j in range(D // tokens):
            g = i * (D // tokens) + j
            out[:, g * D : (g + 1) * D] = acc[j * tokens : (j + 1) * tokens].astype(BF16)


def combine(parts, tokens, width):
    return pl.pallas_call(
        combine_kernel,
        out_shape=jax.ShapeDtypeStruct((tokens, width), BF16),
        compiler_params=pltpu.CompilerParams(vmem_limit_bytes=16 * 2**20),
    )(*parts)


def flip_perm(count, bits):
    return [(i, i ^ bits) for i in range(count)]


def step_perm(count, step):
    return [(i, (i // 8) * 8 + (i % 8 + 2 * step) % 8) for i in range(count)]


def local(
    queries, stretch_keys, stretch_values, cache_keys, cache_values, head_types, sink_blocks, window_blocks
):
    count = lax.axis_size("ctx")
    tables = (head_types, sink_blocks, window_blocks)
    tokens, width = queries.shape
    shard = cache_keys.shape[0]
    own = stretch_keys.shape[0]

    def send(x, perm):
        return lax.ppermute(x, "ctx", perm)

    cut = CUT
    head_part = jnp.concatenate([cache_keys[:cut], cache_values[:cut]], 0)
    tail_part = jnp.concatenate(
        [cache_keys[cut:], stretch_keys, cache_values[cut:], stretch_values], 0
    )
    messages = [(head_part, cut, 0, 0), (tail_part, shard - cut, own, cut)]
    far = [send(message[0], flip_perm(count, 8)) for message in messages]
    steps = [0, 2, 1, 3]
    chunks = [queries] + [send(queries, step_perm(count, s)) for s in steps[1:]]
    sibling = [send(message[0], flip_perm(count, 1)) for message in messages]

    def call(which, sources, state, emit):
        return attend(
            tables, [chunks[i] for i in which], [steps[i] for i in which], sources, shard, state, emit
        )

    def source(array, flip, i):
        return (array, flip) + messages[i][1:]

    near = [source(messages[i][0], 0, i) for i in (0, 1)]
    near += [source(sibling[i], 1, i) for i in (0, 1)]
    others = [1, 2, 3]
    mine = call([0], near, None, False)
    *later, mine = lax.optimization_barrier((*chunks[1:], mine))
    chunks = [queries, *later]
    rest = call(others, near, None, False)
    far0, rest = lax.optimization_barrier((far[0], rest))
    far0_sibling = send(far0, flip_perm(count, 1))
    first = [source(far0, 8, 0), source(far0_sibling, 9, 0)]
    rest = call(others, first, rest, False)
    far1, rest = lax.optimization_barrier((far[1], rest))
    far1_sibling = send(far1, flip_perm(count, 1))
    second = [source(far1, 8, 1), source(far1_sibling, 9, 1)]
    parts = call(others, second, rest, True)
    back = [send(parts[i], step_perm(count, -steps[i + 1])) for i in range(3)]
    mine = call([0], first + second, mine, True)[0]
    return combine([mine] + back, tokens, width)


def solution(mesh):
    placed = (
        P("ctx", "head"),
        P("ctx", "head"),
        P("ctx", "head"),
        P("ctx", "head"),
        P("ctx", "head"),
        P(),
        P(),
        P(),
    )
    return jax.shard_map(
        local, mesh=mesh, in_specs=placed, out_specs=P("ctx", "head"), check_vma=False
    )
```

profile of v0, /device:TPU:16, one launch (start us, length us, event | category | flops | bytes accessed | tf_op | source)
XLA Modules:
  0.0 52.6 jit_solution(8274691329021562769)
XLA Ops:
  0.0 0.0 slice-start.3
  0.0 0.0 copy-start.4
  0.0 0.0 copy-start.5
  0.0 0.0 copy-start.3
  0.1 0.0 copy-start
  0.1 0.0 copy-start.1
  0.1 0.0 copy-start.2
  0.1 0.9 %slice-done = bf16[1536,128]{1,0:T(8,128)(2,1)S(1)} async-done(((bf16[2048,128]{1,0:T(8,128)(2,1)}), bf16[1536,128]{1,0:T(8,128)(2,1)S(1)}, s32[]{:S(2)}) %slice-start) | async-done | bytes 393240 | tf_op jit(solution)/shard_map/slice | solution.py:342
  1.0 0.1 slice-done.2
  1.1 0.1 pad_maximum_fusion.refs_4_.refs_6_
  1.2 0.1 collective-permute-start.4
  1.3 1.6 %collective-permute-start = (bf16[3072,128]{1,0:T(8,128)(2,1)S(1)}, bf16[3072,128]{1,0:T(8,128)(2,1)S(1)}, u32[]{:S(2)}, u32[]{:S(2)}) collective-permute-start(bf16[3072,128]{1,0:T(8,128)(2,1)S(1)} %pad_maximum_fusion.refs_4_.refs_6_), channel_id=1, source_target_pairs={{0,64},{8,72},{16,80},{24,88},{32,96},{40,104},{48,112},{56,120},{... | collective-permute-start | bytes 2359304 | tf_op jit(solution)/shard_map/ppermute | solution.py:339
  2.8 0.0 slice-done.1
  2.8 0.0 slice-done.3
  2.8 0.0 copy-done.4
  2.8 0.0 copy-done.5
  2.9 0.2 collective-permute-start.5
  3.1 0.0 copy-done.3
  3.1 4.1 %collective-permute-start.3 = (bf16[64,1024]{1,0:T(8,128)(2,1)S(1)}, bf16[64,1024]{1,0:T(8,128)(2,1)S(1)}, u32[]{:S(2)}, u32[]{:S(2)}) collective-permute-start(bf16[64,1024]{1,0:T(8,128)(2,1)S(1)} %copy-done.3), channel_id=1, source_target_pairs={{0,48},{8,56},{16,0},{24,8},{32,16},{40,24},{48,32},{56,40},{64,11... | collective-permute-start | bytes 393224 | tf_op jit(solution)/shard_map/ppermute | solution.py:339
  7.2 0.0 collective-permute-start.2
  7.2 0.0 collective-permute-done.5.refs_7_.refs_9_
  7.2 1.9 %collective-permute-start.1 = (bf16[64,1024]{1,0:T(8,128)(2,1)S(1)}, bf16[64,1024]{1,0:T(8,128)(2,1)S(1)}, u32[]{:S(2)}, u32[]{:S(2)}) collective-permute-start(bf16[64,1024]{1,0:T(8,128)(2,1)S(1)} %copy-done.3), channel_id=1, source_target_pairs={{0,32},{8,40},{16,48},{24,56},{32,0},{40,8},{48,16},{56,24},{64,96... | collective-permute-start | bytes 393224 | tf_op jit(solution)/shard_map/ppermute | solution.py:339
  9.0 0.0 collective-permute-done.4.refs_6_.refs_8_
  9.0 0.0 copy-done
  9.0 0.0 copy-done.1
  9.0 0.0 copy-done.2
  9.1 3.4 %shard_map.82.refs_8_ = f32[1,3,512,128]{3,2,1,0:T(8,128)S(1)} custom-call(s32[8]{0:T(128)S(1)} %copy-done, s32[8]{0:T(128)S(1)} %copy-done.1, s32[8]{0:T(128)S(1)} %copy-done.2, bf16[64,1024]{1,0:T(8,128)(2,1)S(1)} %copy-done.3, bf16[3072,128]{1,0:T(8,128)(2,1)S(1)} %pad_maximum_fusion.refs_4_.refs_6_, ...), custom_call_target="tpu_custom_call" | custom-call | flops 1107296256 | bytes 2162688 | tf_op jit(solution)/shard_map/pallas_call | solution.py:273
  12.5 0.0 collective-permute-done.3.refs_5_
  12.5 4.2 %collective-permute-done.2.refs_4_ = bf16[64,1024]{1,0:T(8,128)(2,1)S(1)} collective-permute-done((bf16[64,1024]{1,0:T(8,128)(2,1)S(1)}, bf16[64,1024]{1,0:T(8,128)(2,1)S(1)}, u32[]{:S(2)}, u32[]{:S(2)}) %collective-permute-start.2) | collective-permute-done | bytes 131104 | tf_op jit(solution)/shard_map/ppermute | solution.py:339
  16.6 0.0 collective-permute-done.1.refs_3_
  16.7 9.8 %shard_map.83.refs_8_ = f32[3,3,512,128]{3,2,1,0:T(8,128)S(1)} custom-call(s32[8]{0:T(128)S(1)} %copy-done, s32[8]{0:T(128)S(1)} %copy-done.1, s32[8]{0:T(128)S(1)} %copy-done.2, bf16[64,1024]{1,0:T(8,128)(2,1)S(1)} %collective-permute-done.1.refs_3_, bf16[64,1024]{1,0:T(8,128)(2,1)S(1)} %collective-permute-done.2.refs_4_, ...), custom_call_target="tpu_custom_call" | custom-call | flops 3321888768 | bytes 2162688 | tf_op jit(solution)/shard_map/pallas_call | solution.py:273
  26.5 0.0 collective-permute-done.refs_6_.refs_4_
  26.5 0.1 collective-permute-start.6
  26.6 0.6 %collective-permute-start.7 = (bf16[1152,128]{1,0:T(8,128)(2,1)S(1)}, bf16[1152,128]{1,0:T(8,128)(2,1)S(1)}, u32[]{:S(2)}, u32[]{:S(2)}) collective-permute-start(bf16[1152,128]{1,0:T(8,128)(2,1)S(1)} %pad_maximum_fusion.1.refs_5_.refs_7_), channel_id=1, source_target_pairs={{0,64},{8,72},{16,80},{24,88},{32,96},{40,104},{48,112},{56,120},{... | collective-permute-start | bytes 884744 | tf_op jit(solution)/shard_map/ppermute | solution.py:339
  27.2 1.7 %collective-permute-done.6.refs_7_.refs_5_ = bf16[3072,128]{1,0:T(8,128)(2,1)S(1)} collective-permute-done((bf16[3072,128]{1,0:T(8,128)(2,1)S(1)}, bf16[3072,128]{1,0:T(8,128)(2,1)S(1)}, u32[]{:S(2)}, u32[]{:S(2)}) %collective-permute-start.6) | collective-permute-done | bytes 786464 | tf_op jit(solution)/shard_map/ppermute | solution.py:339
  28.8 7.0 %shard_map.84.refs_8_ = f32[3,3,512,128]{3,2,1,0:T(8,128)S(1)} custom-call(s32[8]{0:T(128)S(1)} %copy-done, s32[8]{0:T(128)S(1)} %copy-done.1, s32[8]{0:T(128)S(1)} %copy-done.2, bf16[64,1024]{1,0:T(8,128)(2,1)S(1)} %collective-permute-done.1.refs_3_, bf16[64,1024]{1,0:T(8,128)(2,1)S(1)} %collective-permute-done.2.refs_4_, ...), custom_call_target="tpu_custom_call" | custom-call | flops 2415919104 | bytes 1572864 | tf_op jit(solution)/shard_map/pallas_call | solution.py:273
  35.8 0.2 collective-permute-done.7.refs_6_
  36.0 0.1 collective-permute-start.8
  36.0 1.5 %collective-permute-done.8.refs_7_ = bf16[1152,128]{1,0:T(8,128)(2,1)S(1)} collective-permute-done((bf16[1152,128]{1,0:T(8,128)(2,1)S(1)}, bf16[1152,128]{1,0:T(8,128)(2,1)S(1)}, u32[]{:S(2)}, u32[]{:S(2)}) %collective-permute-start.8) | collective-permute-done | bytes 294944 | tf_op jit(solution)/shard_map/ppermute | solution.py:339
  37.6 4.1 %shard_map.86 = bf16[3,528,128]{2,1,0:T(8,128)(2,1)S(1)} custom-call(s32[8]{0:T(128)S(1)} %copy-done, s32[8]{0:T(128)S(1)} %copy-done.1, s32[8]{0:T(128)S(1)} %copy-done.2, bf16[64,1024]{1,0:T(8,128)(2,1)S(1)} %collective-permute-done.1.refs_3_, bf16[64,1024]{1,0:T(8,128)(2,1)S(1)} %collective-permute-done.2.refs_4_, ...), custom_call_target="tpu_custom_call" | custom-call | flops 905969664 | bytes 589824 | tf_op jit(solution)/shard_map/pallas_call | solution.py:273
  41.7 0.1 collective-permute-start.11
  41.8 3.2 %collective-permute-start.10 = (bf16[528,128]{1,0:T(8,128)(2,1)S(1)}, bf16[528,128]{1,0:T(8,128)(2,1)S(1)}, u32[]{:S(2)}, u32[]{:S(2)}) collective-permute-start(bf16[528,128]{1,0:T(8,128)(2,1)S(1)} %get-tuple-element.22), channel_id=1, source_target_pairs={{0,48},{8,56},{16,0},{24,8},{32,16},{40,24},{48,32},{56,40},{64,11... | collective-permute-start | bytes 405512 | tf_op jit(solution)/shard_map/ppermute | solution.py:339
  45.0 0.0 collective-permute-start.9
  45.0 3.3 %shard_map.85 = bf16[1,528,128]{2,1,0:T(8,128)(2,1)S(1)} custom-call(s32[8]{0:T(128)S(1)} %copy-done, s32[8]{0:T(128)S(1)} %copy-done.1, s32[8]{0:T(128)S(1)} %copy-done.2, bf16[64,1024]{1,0:T(8,128)(2,1)S(1)} %copy-done.3, bf16[3072,128]{1,0:T(8,128)(2,1)S(1)} %collective-permute-done.refs_6_.refs_4_, ...), custom_call_target="tpu_custom_call" | custom-call | flops 1107296256 | bytes 2162688 | tf_op jit(solution)/shard_map/pallas_call | solution.py:273
  48.4 0.3 collective-permute-done.11.refs_3_
  48.6 2.2 %collective-permute-done.10.refs_2_ = bf16[528,128]{1,0:T(8,128)(2,1)S(1)} collective-permute-done((bf16[528,128]{1,0:T(8,128)(2,1)S(1)}, bf16[528,128]{1,0:T(8,128)(2,1)S(1)}, u32[]{:S(2)}, u32[]{:S(2)}) %collective-permute-start.10) | collective-permute-done | bytes 135200 | tf_op jit(solution)/shard_map/ppermute | solution.py:339
  50.8 0.8 %collective-permute-done.9.refs_1_ = bf16[528,128]{1,0:T(8,128)(2,1)S(1)} collective-permute-done((bf16[528,128]{1,0:T(8,128)(2,1)S(1)}, bf16[528,128]{1,0:T(8,128)(2,1)S(1)}, u32[]{:S(2)}, u32[]{:S(2)}) %collective-permute-start.9) | collective-permute-done | bytes 135200 | tf_op jit(solution)/shard_map/ppermute | solution.py:339
  51.6 1.0 %shard_map.87 = bf16[64,1024]{1,0:T(8,128)(2,1)} custom-call(bf16[528,128]{1,0:T(8,128)(2,1)S(1)} %bitcast.7, bf16[528,128]{1,0:T(8,128)(2,1)S(1)} %collective-permute-done.9.refs_1_, bf16[528,128]{1,0:T(8,128)(2,1)S(1)} %collective-permute-done.10.refs_2_, bf16[528,128]{1,0:T(8,128)(2,1)S(1)} %collective-permute-done.11.refs_3_), custom_call_target="tpu_custom_call" | custom-call | tf_op jit(solution)/shard_map/pallas_call | solution.py:314
  (5 shorter events, 0.1 us)
Async XLA Ops:
  0.0 1.0 %slice-start = ((bf16[2048,128]{1,0:T(8,128)(2,1)}), bf16[1536,128]{1,0:T(8,128)(2,1)S(1)}, s32[]{:S(2)}) async-start(bf16[2048,128]{1,0:T(8,128)(2,1)} %param.11), calls=%async_computation | async-start | bytes 786432 | tf_op jit(solution)/shard_map/slice | solution.py:342
  0.0 1.1 %slice-start.2 = ((bf16[2048,128]{1,0:T(8,128)(2,1)}), bf16[1536,128]{1,0:T(8,128)(2,1)S(1)}, s32[]{:S(2)}) async-start(bf16[2048,128]{1,0:T(8,128)(2,1)} %param.12), calls=%async_computation.2 | async-start | bytes 786432 | tf_op jit(solution)/shard_map/slice | solution.py:342
  0.0 2.8 %slice-start.1 = ((bf16[2048,128]{1,0:T(8,128)(2,1)}), bf16[512,128]{1,0:T(8,128)(2,1)S(1)}, s32[]{:S(2)}) async-start(bf16[2048,128]{1,0:T(8,128)(2,1)} %param.11), calls=%async_computation.1 | async-start | bytes 262144 | tf_op jit(solution)/shard_map/slice | solution.py:344
  0.0 2.8 %slice-start.3 = ((bf16[2048,128]{1,0:T(8,128)(2,1)}), bf16[512,128]{1,0:T(8,128)(2,1)S(1)}, s32[]{:S(2)}) async-start(bf16[2048,128]{1,0:T(8,128)(2,1)} %param.12), calls=%async_computation.3 | async-start | bytes 262144 | tf_op jit(solution)/shard_map/slice | solution.py:344
  0.0 2.8 %copy-start.4 = (bf16[64,128]{1,0:T(8,128)(2,1)S(1)}, bf16[64,128]{1,0:T(8,128)(2,1)}, u32[]{:S(2)}) copy-start(bf16[64,128]{1,0:T(8,128)(2,1)} %param.10) | copy-start | bytes 49156
  0.0 2.8 %copy-start.5 = (bf16[64,128]{1,0:T(8,128)(2,1)S(1)}, bf16[64,128]{1,0:T(8,128)(2,1)}, u32[]{:S(2)}) copy-start(bf16[64,128]{1,0:T(8,128)(2,1)} %param.9) | copy-start | bytes 49156
  0.0 3.1 %copy-start.3 = (bf16[64,1024]{1,0:T(8,128)(2,1)S(1)}, bf16[64,1024]{1,0:T(8,128)(2,1)}, u32[]{:S(2)}) copy-start(bf16[64,1024]{1,0:T(8,128)(2,1)} %refs_3_.3) | copy-start | bytes 393220
  0.1 9.0 %copy-start = (s32[8]{0:T(128)S(1)}, s32[8]{0:T(128)}, u32[]{:S(2)}) copy-start(s32[8]{0:T(128)} %refs_0_.9) | copy-start | bytes 100
  0.1 9.0 %copy-start.1 = (s32[8]{0:T(128)S(1)}, s32[8]{0:T(128)}, u32[]{:S(2)}) copy-start(s32[8]{0:T(128)} %refs_1_.9) | copy-start | bytes 100
  0.1 9.0 %copy-start.2 = (s32[8]{0:T(128)S(1)}, s32[8]{0:T(128)}, u32[]{:S(2)}) copy-start(s32[8]{0:T(128)} %refs_2_.9) | copy-start | bytes 100
  1.2 7.9 %collective-permute-start.4 = (bf16[3072,128]{1,0:T(8,128)(2,1)S(1)}, bf16[3072,128]{1,0:T(8,128)(2,1)S(1)}, u32[]{:S(2)}, u32[]{:S(2)}) collective-permute-start(bf16[3072,128]{1,0:T(8,128)(2,1)S(1)} %pad_maximum_fusion.refs_4_.refs_6_), channel_id=1, source_target_pairs={{0,8},{8,0},{16,24},{24,16},{32,40},{40,32},{48,56},{56,48},{64,72... | collective-permute-start | bytes 2359304 | tf_op jit(solution)/shard_map/ppermute | solution.py:339
  1.3 25.2 %collective-permute-start = (bf16[3072,128]{1,0:T(8,128)(2,1)S(1)}, bf16[3072,128]{1,0:T(8,128)(2,1)S(1)}, u32[]{:S(2)}, u32[]{:S(2)}) collective-permute-start(bf16[3072,128]{1,0:T(8,128)(2,1)S(1)} %pad_maximum_fusion.refs_4_.refs_6_), channel_id=1, source_target_pairs={{0,64},{8,72},{16,80},{24,88},{32,96},{40,104},{48,112},{56,120},{... | collective-permute-start | bytes 2359304 | tf_op jit(solution)/shard_map/ppermute | solution.py:339
  2.9 4.3 %collective-permute-start.5 = (bf16[1152,128]{1,0:T(8,128)(2,1)S(1)}, bf16[1152,128]{1,0:T(8,128)(2,1)S(1)}, u32[]{:S(2)}, u32[]{:S(2)}) collective-permute-start(bf16[1152,128]{1,0:T(8,128)(2,1)S(1)} %pad_maximum_fusion.1.refs_5_.refs_7_), channel_id=1, source_target_pairs={{0,8},{8,0},{16,24},{24,16},{32,40},{40,32},{48,56},{56,48},{64,72... | collective-permute-start | bytes 884744 | tf_op jit(solution)/shard_map/ppermute | solution.py:339
  3.1 9.4 %collective-permute-start.3 = (bf16[64,1024]{1,0:T(8,128)(2,1)S(1)}, bf16[64,1024]{1,0:T(8,128)(2,1)S(1)}, u32[]{:S(2)}, u32[]{:S(2)}) collective-permute-start(bf16[64,1024]{1,0:T(8,128)(2,1)S(1)} %copy-done.3), channel_id=1, source_target_pairs={{0,48},{8,56},{16,0},{24,8},{32,16},{40,24},{48,32},{56,40},{64,11... | collective-permute-start | bytes 393224 | tf_op jit(solution)/shard_map/ppermute | solution.py:339
  7.2 9.5 %collective-permute-start.2 = (bf16[64,1024]{1,0:T(8,128)(2,1)S(1)}, bf16[64,1024]{1,0:T(8,128)(2,1)S(1)}, u32[]{:S(2)}, u32[]{:S(2)}) collective-permute-start(bf16[64,1024]{1,0:T(8,128)(2,1)S(1)} %copy-done.3), channel_id=1, source_target_pairs={{0,16},{8,24},{16,32},{24,40},{32,48},{40,56},{48,0},{56,8},{64,80... | collective-permute-start | bytes 393224 | tf_op jit(solution)/shard_map/ppermute | solution.py:339
  7.2 9.5 %collective-permute-start.1 = (bf16[64,1024]{1,0:T(8,128)(2,1)S(1)}, bf16[64,1024]{1,0:T(8,128)(2,1)S(1)}, u32[]{:S(2)}, u32[]{:S(2)}) collective-permute-start(bf16[64,1024]{1,0:T(8,128)(2,1)S(1)} %copy-done.3), channel_id=1, source_target_pairs={{0,32},{8,40},{16,48},{24,56},{32,0},{40,8},{48,16},{56,24},{64,96... | collective-permute-start | bytes 393224 | tf_op jit(solution)/shard_map/ppermute | solution.py:339
  26.5 2.4 %collective-permute-start.6 = (bf16[3072,128]{1,0:T(8,128)(2,1)S(1)}, bf16[3072,128]{1,0:T(8,128)(2,1)S(1)}, u32[]{:S(2)}, u32[]{:S(2)}) collective-permute-start(bf16[3072,128]{1,0:T(8,128)(2,1)S(1)} %collective-permute-done.refs_6_.refs_4_), channel_id=1, source_target_pairs={{0,8},{8,0},{16,24},{24,16},{32,40},{40,32},{48,56},{56,48},{64,72... | collective-permute-start | bytes 2359304 | tf_op jit(solution)/shard_map/ppermute | solution.py:339
  26.6 9.4 %collective-permute-start.7 = (bf16[1152,128]{1,0:T(8,128)(2,1)S(1)}, bf16[1152,128]{1,0:T(8,128)(2,1)S(1)}, u32[]{:S(2)}, u32[]{:S(2)}) collective-permute-start(bf16[1152,128]{1,0:T(8,128)(2,1)S(1)} %pad_maximum_fusion.1.refs_5_.refs_7_), channel_id=1, source_target_pairs={{0,64},{8,72},{16,80},{24,88},{32,96},{40,104},{48,112},{56,120},{... | collective-permute-start | bytes 884744 | tf_op jit(solution)/shard_map/ppermute | solution.py:339
  36.0 1.6 %collective-permute-start.8 = (bf16[1152,128]{1,0:T(8,128)(2,1)S(1)}, bf16[1152,128]{1,0:T(8,128)(2,1)S(1)}, u32[]{:S(2)}, u32[]{:S(2)}) collective-permute-start(bf16[1152,128]{1,0:T(8,128)(2,1)S(1)} %collective-permute-done.7.refs_6_), channel_id=1, source_target_pairs={{0,8},{8,0},{16,24},{24,16},{32,40},{40,32},{48,56},{56,48},{64,72... | collective-permute-start | bytes 884744 | tf_op jit(solution)/shard_map/ppermute | solution.py:339
  41.7 6.9 %collective-permute-start.11 = (bf16[528,128]{1,0:T(8,128)(2,1)S(1)}, bf16[528,128]{1,0:T(8,128)(2,1)S(1)}, u32[]{:S(2)}, u32[]{:S(2)}) collective-permute-start(bf16[528,128]{1,0:T(8,128)(2,1)S(1)} %get-tuple-element.21), channel_id=1, source_target_pairs={{0,16},{8,24},{16,32},{24,40},{32,48},{40,56},{48,0},{56,8},{64,80... | collective-permute-start | bytes 405512 | tf_op jit(solution)/shard_map/ppermute | solution.py:339
  41.8 9.0 %collective-permute-start.10 = (bf16[528,128]{1,0:T(8,128)(2,1)S(1)}, bf16[528,128]{1,0:T(8,128)(2,1)S(1)}, u32[]{:S(2)}, u32[]{:S(2)}) collective-permute-start(bf16[528,128]{1,0:T(8,128)(2,1)S(1)} %get-tuple-element.22), channel_id=1, source_target_pairs={{0,48},{8,56},{16,0},{24,8},{32,16},{40,24},{48,32},{56,40},{64,11... | collective-permute-start | bytes 405512 | tf_op jit(solution)/shard_map/ppermute | solution.py:339
  45.0 6.6 %collective-permute-start.9 = (bf16[528,128]{1,0:T(8,128)(2,1)S(1)}, bf16[528,128]{1,0:T(8,128)(2,1)S(1)}, u32[]{:S(2)}, u32[]{:S(2)}) collective-permute-start(bf16[528,128]{1,0:T(8,128)(2,1)S(1)} %get-tuple-element.23), channel_id=1, source_target_pairs={{0,32},{8,40},{16,48},{24,56},{32,0},{40,8},{48,16},{56,24},{64,96... | collective-permute-start | bytes 405512 | tf_op jit(solution)/shard_map/ppermute | solution.py:339
where the time goes:
time: 52.8 us; the launch traced here: 52.6 us
  Pallas kernels  28.7 us (54%)
  starting transfers between devices  11.9 us (23%)
  waiting for transfers between devices  10.8 us (20%)
  local copies, waits for them, and re-layouts  1.1 us (2%)
    pallas_call x5, Pallas kernels, attend(): pl.pallas_call(functools.partial(attend_kernel, geom), out_shape=out_shap...  27.6 us
    ppermute x12, starting transfers between devices, send(): return lax.ppermute(x, 'ctx', perm)  11.9 us
    ppermute x12, waiting for transfers between devices, send(): return lax.ppermute(x, 'ctx', perm)  10.8 us
  transfers between devices with their start and end apart: 12, of which 7 were waited for; matrix products, arithmetic and copies ran while one was open for 0% of the time, Pallas kernels for 45%

commit v1 on v0

--- a/solution.py
+++ b/solution.py
@@ -42,8 +42,7 @@
     q_in = refs[3 : 3 + n]
     kv = refs[3 + n : 3 + n + n_src]
     rest = refs[3 + n + n_src :]
-    if state_in:
-        old, rest = rest[0], rest[1:]
+    old, rest = rest[: len(state_in)], rest[len(state_in) :]
     out, q_buf = rest[0], rest[1]
     state = rest[2] if emit else out
     group = q_in[0].shape[1] // D
@@ -82,15 +81,22 @@
         x = scores_of(q_buf[c], jnp.concatenate(keys, 0)) * SCALE
         return x, jnp.concatenate(values, 0), key_pos <= token + owner * tokens
 
+    places = [(ref, j) for ref, size in zip(old, state_in) for j in range(size)]
+
+    def restore():
+        for c in range(n):
+            if state_in:
+                ref, j = places[c]
+                for i in range(3):
+                    state[c, i] = ref[j, i]
+            else:
+                state[c, 0] = jnp.full((q_rows, D), NEG, F32)
+                for i in (1, 2):
+                    state[c, i] = jnp.zeros((q_rows, D), F32)
+
+    begin = old[0] if len(state_in) == 1 else state
+
     def exact(c):
-        if state_in:
-            for i in range(3):
-                state[c, i] = old[c, i]
-        else:
-            state[c, 0] = jnp.full((q_rows, D), NEG, F32)
-            state[c, 1] = jnp.zeros((q_rows, D), F32)
-            state[c, 2] = jnp.zeros((q_rows, D), F32)
-
         def update(x, values, mask):
             before = state[c, 0]
             if mask is not None:
@@ -158,7 +164,7 @@
                     x = x * SCALE
                 if i == 1 or segments[i - 2][0] != c:
                     if state_in:
-                        fixed[c], total[c], acc[c] = (old[chosen[c], k] for k in range(3))
+                        fixed[c], total[c], acc[c] = (begin[chosen[c], k] for k in range(3))
                     else:
                         fixed[c] = row_max(x[:, :SAMPLE]) + HEADROOM
                 weights = []
@@ -187,8 +193,9 @@
 
             lax.fori_loop(0, n, step, 0)
 
-    @pl.when(kind == 1)
-    def _():
+    def quick():
+        if len(state_in) > 1:
+            restore()
         if n == 1 or UNROLL:
             fixed_stabiliser(list(range(n)))
         else:
@@ -199,14 +206,13 @@
 
             lax.fori_loop(0, n, one, 0)
         flags = [jnp.where(state[c, 1] < SAFE, 0.0, 1.0) for c in range(n)]
-        safe = jnp.max(functools.reduce(jnp.maximum, flags)) < 0.5
-
-        @pl.when(jnp.logical_not(safe))
-        def _():
-            every_exact()
-
-    @pl.when(kind != 1)
+        return jnp.where(jnp.max(functools.reduce(jnp.maximum, flags)) < 0.5, 0, 1)
+
+    left_over = lax.cond(kind == 1, quick, lambda: jnp.int32(1))
+
+    @pl.when(left_over == 1)
     def _():
+        restore()
         every_exact()
 
     if emit:
@@ -247,7 +253,7 @@
     return (ctx // 8) * 8 + (ctx % 8 - 2 * step + 8) % 8
 
 
-def attend(tables, queries, steps, sources, shard, state, emit):
+def attend(tables, queries, steps, sources, shard, states, emit):
     n = len(steps)
     tokens, width = queries[0].shape
     q_rows = tokens * (width // D)
@@ -256,7 +262,7 @@
         tuple(source[1:] for source in sources),
         shard,
         lax.axis_size("ctx"),
-        state is not None,
+        tuple(array.shape[0] for array in states),
         emit,
     )
     shape_state = (n, 3, q_rows, D)
@@ -268,7 +274,6 @@
         scratch = [pltpu.VMEM((n, q_rows, D), BF16)]
     smem = pl.BlockSpec(memory_space=pltpu.SMEM)
     vmem = pl.BlockSpec(memory_space=pltpu.VMEM)
-    states = [] if state is None else [state]
     pairs = n * q_rows * sum(source[2] + source[3] for source in sources)
     return pl.pallas_call(
         functools.partial(attend_kernel, geom),
@@ -345,13 +350,13 @@
     )
     messages = [(head_part, cut, 0, 0), (tail_part, shard - cut, own, cut)]
     far = [send(message[0], flip_perm(count, 8)) for message in messages]
-    steps = [0, 2, 1, 3]
+    steps = [0, 3, 1, 2]
     chunks = [queries] + [send(queries, step_perm(count, s)) for s in steps[1:]]
     sibling = [send(message[0], flip_perm(count, 1)) for message in messages]
 
-    def call(which, sources, state, emit):
+    def call(which, sources, states, emit):
         return attend(
-            tables, [chunks[i] for i in which], [steps[i] for i in which], sources, shard, state, emit
+            tables, [chunks[i] for i in which], [steps[i] for i in which], sources, shard, states, emit
         )
 
     def source(array, flip, i):
@@ -360,20 +365,21 @@
     near = [source(messages[i][0], 0, i) for i in (0, 1)]
     near += [source(sibling[i], 1, i) for i in (0, 1)]
     others = [1, 2, 3]
-    mine = call([0], near, None, False)
-    *later, mine = lax.optimization_barrier((*chunks[1:], mine))
-    chunks = [queries, *later]
-    rest = call(others, near, None, False)
-    far0, rest = lax.optimization_barrier((far[0], rest))
+    mine = call([0], near, [], False)
+    chunks[1], mine = lax.optimization_barrier((chunks[1], mine))
+    left = call([1], near, [], False)
+    chunks[2], chunks[3], left = lax.optimization_barrier((*chunks[2:], left))
+    right = call([2, 3], near, [], False)
+    far0, right = lax.optimization_barrier((far[0], right))
     far0_sibling = send(far0, flip_perm(count, 1))
     first = [source(far0, 8, 0), source(far0_sibling, 9, 0)]
-    rest = call(others, first, rest, False)
+    rest = call(others, first, [left, right], False)
     far1, rest = lax.optimization_barrier((far[1], rest))
     far1_sibling = send(far1, flip_perm(count, 1))
     second = [source(far1, 8, 1), source(far1_sibling, 9, 1)]
-    parts = call(others, second, rest, True)
+    parts = call(others, second, [rest], True)
     back = [send(parts[i], step_perm(count, -steps[i + 1])) for i in range(3)]
-    mine = call([0], first + second, mine, True)[0]
+    mine = call([0], first + second, [mine], True)[0]
     return combine([mine] + back, tokens, width)
 
 

time: 52.8 us -> 51.5 us (0.975)
  waiting for transfers between devices: 10.8 us -> 7.98 us
  starting transfers between devices: 11.9 us -> 12.6 us
  Pallas kernels: 28.7 us -> 29.3 us
    ppermute x12, waiting for transfers between devices: 10.8 us -> 7.98 us  [send(): return lax.ppermute(x, 'ctx', perm)]
    ppermute x12, starting transfers between devices: 11.9 us -> 12.6 us  [send(): return lax.ppermute(x, 'ctx', perm)]
    pallas_call x5 -> x6, Pallas kernels: 27.6 us -> 28.3 us  [attend(): pl.pallas_call(functools.partial(attend_kernel, geom), out_shape=out_shap...]
  transfers between devices with their start and end apart: 12 -> 12, of which waited for: 7 -> 5; matrix products, arithmetic and copies ran while one was open for 0% -> 0% of each run, Pallas kernels for 45% -> 47%
where the time goes in v1:
time: 51.5 us; the launch traced here: 51.2 us
  Pallas kernels  29.3 us (57%)
  starting transfers between devices  12.6 us (24%)
  waiting for transfers between devices  7.98 us (15%)
  local copies, waits for them, and re-layouts  1.1 us (2%)
    pallas_call x6, Pallas kernels, attend(): pl.pallas_call(functools.partial(attend_kernel, geom), out_shape=out_shap...  28.3 us
    ppermute x12, starting transfers between devices, send(): return lax.ppermute(x, 'ctx', perm)  12.6 us
    ppermute x12, waiting for transfers between devices, send(): return lax.ppermute(x, 'ctx', perm)  7.98 us
    slice x4, local copies, waits for them, and re-layouts, local(): head_part = jnp.concatenate([cache_keys[:cut], cache_values[:cut]], 0)  1.04 us
  transfers between devices with their start and end apart: 12, of which 5 were waited for; matrix products, arithmetic and copies ran while one was open for 0% of the time, Pallas kernels for 47%

profile of v1, /device:TPU:16, one launch (start us, length us, event | category | flops | bytes accessed | tf_op | source)
XLA Modules:
  0.0 51.2 jit_solution(15340322971364103107)
XLA Ops:
  0.0 0.0 slice-start.3
  0.0 0.0 copy-start.4
  0.0 0.0 copy-start.5
  0.0 0.0 copy-start.3
  0.1 0.0 copy-start
  0.1 0.0 copy-start.1
  0.1 0.0 copy-start.2
  0.1 0.9 %slice-done = bf16[1536,128]{1,0:T(8,128)(2,1)S(1)} async-done(((bf16[2048,128]{1,0:T(8,128)(2,1)}), bf16[1536,128]{1,0:T(8,128)(2,1)S(1)}, s32[]{:S(2)}) %slice-start) | async-done | bytes 393240 | tf_op jit(solution)/shard_map/slice | solution.py:347
  1.0 0.1 slice-done.2
  1.1 0.1 pad_maximum_fusion.refs_4_.refs_5_
  1.2 0.1 collective-permute-start.4
  1.3 1.6 %collective-permute-start = (bf16[3072,128]{1,0:T(8,128)(2,1)S(1)}, bf16[3072,128]{1,0:T(8,128)(2,1)S(1)}, u32[]{:S(2)}, u32[]{:S(2)}) collective-permute-start(bf16[3072,128]{1,0:T(8,128)(2,1)S(1)} %pad_maximum_fusion.refs_4_.refs_5_), channel_id=1, source_target_pairs={{0,64},{8,72},{16,80},{24,88},{32,96},{40,104},{48,112},{56,120},{... | collective-permute-start | bytes 2359304 | tf_op jit(solution)/shard_map/ppermute | solution.py:344
  2.8 0.0 slice-done.1
  2.8 0.0 slice-done.3
  2.8 0.0 copy-done.4
  2.8 0.0 copy-done.5
  2.9 0.2 collective-permute-start.5
  3.1 0.0 copy-done.3
  3.1 4.1 %collective-permute-start.3 = (bf16[64,1024]{1,0:T(8,128)(2,1)S(1)}, bf16[64,1024]{1,0:T(8,128)(2,1)S(1)}, u32[]{:S(2)}, u32[]{:S(2)}) collective-permute-start(bf16[64,1024]{1,0:T(8,128)(2,1)S(1)} %copy-done.3), channel_id=1, source_target_pairs={{0,48},{8,56},{16,0},{24,8},{32,16},{40,24},{48,32},{56,40},{64,11... | collective-permute-start | bytes 393224 | tf_op jit(solution)/shard_map/ppermute | solution.py:344
  7.2 0.0 collective-permute-start.2
  7.2 0.0 collective-permute-done.5.refs_7_.refs_8_
  7.2 1.3 %collective-permute-start.1 = (bf16[64,1024]{1,0:T(8,128)(2,1)S(1)}, bf16[64,1024]{1,0:T(8,128)(2,1)S(1)}, u32[]{:S(2)}, u32[]{:S(2)}) collective-permute-start(bf16[64,1024]{1,0:T(8,128)(2,1)S(1)} %copy-done.3), channel_id=1, source_target_pairs={{0,16},{8,24},{16,32},{24,40},{32,48},{40,56},{48,0},{56,8},{64,80... | collective-permute-start | bytes 393224 | tf_op jit(solution)/shard_map/ppermute | solution.py:344
  8.4 0.0 collective-permute-done.4.refs_6_.refs_7_
  8.4 0.0 copy-done
  8.4 0.0 copy-done.1
  8.4 3.4 %shard_map.82.refs_8_ = f32[1,3,512,128]{3,2,1,0:T(8,128)S(1)} custom-call(s32[8]{0:T(128)S(1)} %copy-done, s32[8]{0:T(128)S(1)} %copy-done.1, s32[8]{0:T(128)S(1)} %copy-done.2, bf16[64,1024]{1,0:T(8,128)(2,1)S(1)} %copy-done.3, bf16[3072,128]{1,0:T(8,128)(2,1)S(1)} %pad_maximum_fusion.refs_4_.refs_5_, ...), custom_call_target="tpu_custom_call" | custom-call | flops 1107296256 | bytes 2162688 | tf_op jit(solution)/shard_map/pallas_call | solution.py:278
  11.9 1.4 %collective-permute-done.3.refs_3_ = bf16[64,1024]{1,0:T(8,128)(2,1)S(1)} collective-permute-done((bf16[64,1024]{1,0:T(8,128)(2,1)S(1)}, bf16[64,1024]{1,0:T(8,128)(2,1)S(1)}, u32[]{:S(2)}, u32[]{:S(2)}) %collective-permute-start.3) | collective-permute-done | bytes 131104 | tf_op jit(solution)/shard_map/ppermute | solution.py:344
  13.2 3.6 %shard_map.83.refs_8_ = f32[1,3,512,128]{3,2,1,0:T(8,128)S(1)} custom-call(s32[8]{0:T(128)S(1)} %copy-done, s32[8]{0:T(128)S(1)} %copy-done.1, s32[8]{0:T(128)S(1)} %copy-done.2, bf16[64,1024]{1,0:T(8,128)(2,1)S(1)} %collective-permute-done.3.refs_3_, bf16[3072,128]{1,0:T(8,128)(2,1)S(1)} %pad_maximum_fusion.refs_4_.refs_5_, ...), custom_call_target="tpu_custom_call" | custom-call | flops 1107296256 | bytes 2162688 | tf_op jit(solution)/shard_map/pallas_call | solution.py:278
  16.9 0.0 collective-permute-done.2.refs_4_.refs_5_
  16.9 0.0 collective-permute-done.1.refs_3_.refs_4_
  16.9 6.6 %shard_map.84.refs_9_ = f32[2,3,512,128]{3,2,1,0:T(8,128)S(1)} custom-call(s32[8]{0:T(128)S(1)} %copy-done, s32[8]{0:T(128)S(1)} %copy-done.1, s32[8]{0:T(128)S(1)} %copy-done.2, bf16[64,1024]{1,0:T(8,128)(2,1)S(1)} %collective-permute-done.1.refs_3_.refs_4_, bf16[64,1024]{1,0:T(8,128)(2,1)S(1)} %collective-permute-done.2.refs_4_.refs_5_, ...), custom_call_target="tpu_custom_call" | custom-call | flops 2214592512 | bytes 2162688 | tf_op jit(solution)/shard_map/pallas_call | solution.py:278
  23.5 0.0 collective-permute-done.refs_6_.refs_4_
  23.5 0.1 collective-permute-start.6
  23.6 0.6 %collective-permute-start.7 = (bf16[1152,128]{1,0:T(8,128)(2,1)S(1)}, bf16[1152,128]{1,0:T(8,128)(2,1)S(1)}, u32[]{:S(2)}, u32[]{:S(2)}) collective-permute-start(bf16[1152,128]{1,0:T(8,128)(2,1)S(1)} %pad_maximum_fusion.1.refs_5_.refs_6_), channel_id=1, source_target_pairs={{0,64},{8,72},{16,80},{24,88},{32,96},{40,104},{48,112},{56,120},{... | collective-permute-start | bytes 884744 | tf_op jit(solution)/shard_map/ppermute | solution.py:344
  24.2 1.7 %collective-permute-done.6.refs_7_.refs_5_ = bf16[3072,128]{1,0:T(8,128)(2,1)S(1)} collective-permute-done((bf16[3072,128]{1,0:T(8,128)(2,1)S(1)}, bf16[3072,128]{1,0:T(8,128)(2,1)S(1)}, u32[]{:S(2)}, u32[]{:S(2)}) %collective-permute-start.6) | collective-permute-done | bytes 786464 | tf_op jit(solution)/shard_map/ppermute | solution.py:344
  25.9 7.0 %shard_map.85.refs_8_ = f32[3,3,512,128]{3,2,1,0:T(8,128)S(1)} custom-call(s32[8]{0:T(128)S(1)} %copy-done, s32[8]{0:T(128)S(1)} %copy-done.1, s32[8]{0:T(128)S(1)} %copy-done.2, bf16[64,1024]{1,0:T(8,128)(2,1)S(1)} %collective-permute-done.3.refs_3_, bf16[64,1024]{1,0:T(8,128)(2,1)S(1)} %collective-permute-done.1.refs_3_.refs_4_, ...), custom_call_target="tpu_custom_call" | custom-call | flops 2415919104 | bytes 1572864 | tf_op jit(solution)/shard_map/pallas_call | solution.py:278
  32.9 0.2 collective-permute-done.7.refs_6_
  33.0 0.0 collective-permute-start.8
  33.1 1.5 %collective-permute-done.8.refs_7_ = bf16[1152,128]{1,0:T(8,128)(2,1)S(1)} collective-permute-done((bf16[1152,128]{1,0:T(8,128)(2,1)S(1)}, bf16[1152,128]{1,0:T(8,128)(2,1)S(1)}, u32[]{:S(2)}, u32[]{:S(2)}) %collective-permute-start.8) | collective-permute-done | bytes 294944 | tf_op jit(solution)/shard_map/ppermute | solution.py:344
  34.6 4.4 %shard_map.87 = bf16[3,528,128]{2,1,0:T(8,128)(2,1)S(1)} custom-call(s32[8]{0:T(128)S(1)} %copy-done, s32[8]{0:T(128)S(1)} %copy-done.1, s32[8]{0:T(128)S(1)} %copy-done.2, bf16[64,1024]{1,0:T(8,128)(2,1)S(1)} %collective-permute-done.3.refs_3_, bf16[64,1024]{1,0:T(8,128)(2,1)S(1)} %collective-permute-done.1.refs_3_.refs_4_, ...), custom_call_target="tpu_custom_call" | custom-call | flops 905969664 | bytes 589824 | tf_op jit(solution)/shard_map/pallas_call | solution.py:278
  39.0 1.5 %collective-permute-start.11 = (bf16[528,128]{1,0:T(8,128)(2,1)S(1)}, bf16[528,128]{1,0:T(8,128)(2,1)S(1)}, u32[]{:S(2)}, u32[]{:S(2)}) collective-permute-start(bf16[528,128]{1,0:T(8,128)(2,1)S(1)} %get-tuple-element.23), channel_id=1, source_target_pairs={{0,32},{8,40},{16,48},{24,56},{32,0},{40,8},{48,16},{56,24},{64,96... | collective-permute-start | bytes 405512 | tf_op jit(solution)/shard_map/ppermute | solution.py:344
  40.6 2.3 %collective-permute-start.10 = (bf16[528,128]{1,0:T(8,128)(2,1)S(1)}, bf16[528,128]{1,0:T(8,128)(2,1)S(1)}, u32[]{:S(2)}, u32[]{:S(2)}) collective-permute-start(bf16[528,128]{1,0:T(8,128)(2,1)S(1)} %get-tuple-element.24), channel_id=1, source_target_pairs={{0,48},{8,56},{16,0},{24,8},{32,16},{40,24},{48,32},{56,40},{64,11... | collective-permute-start | bytes 405512 | tf_op jit(solution)/shard_map/ppermute | solution.py:344
  42.9 0.8 %collective-permute-start.9 = (bf16[528,128]{1,0:T(8,128)(2,1)S(1)}, bf16[528,128]{1,0:T(8,128)(2,1)S(1)}, u32[]{:S(2)}, u32[]{:S(2)}) collective-permute-start(bf16[528,128]{1,0:T(8,128)(2,1)S(1)} %get-tuple-element.25), channel_id=1, source_target_pairs={{0,16},{8,24},{16,32},{24,40},{32,48},{40,56},{48,0},{56,8},{64,80... | collective-permute-start | bytes 405512 | tf_op jit(solution)/shard_map/ppermute | solution.py:344
  43.6 3.3 %shard_map.86 = bf16[1,528,128]{2,1,0:T(8,128)(2,1)S(1)} custom-call(s32[8]{0:T(128)S(1)} %copy-done, s32[8]{0:T(128)S(1)} %copy-done.1, s32[8]{0:T(128)S(1)} %copy-done.2, bf16[64,1024]{1,0:T(8,128)(2,1)S(1)} %copy-done.3, bf16[3072,128]{1,0:T(8,128)(2,1)S(1)} %collective-permute-done.refs_6_.refs_4_, ...), custom_call_target="tpu_custom_call" | custom-call | flops 1107296256 | bytes 2162688 | tf_op jit(solution)/shard_map/pallas_call | solution.py:278
  47.0 0.0 collective-permute-done.11.refs_3_
  47.0 3.2 %collective-permute-done.10.refs_2_ = bf16[528,128]{1,0:T(8,128)(2,1)S(1)} collective-permute-done((bf16[528,128]{1,0:T(8,128)(2,1)S(1)}, bf16[528,128]{1,0:T(8,128)(2,1)S(1)}, u32[]{:S(2)}, u32[]{:S(2)}) %collective-permute-start.10) | collective-permute-done | bytes 135200 | tf_op jit(solution)/shard_map/ppermute | solution.py:344
  50.2 0.0 collective-permute-done.9.refs_1_
  50.2 1.0 %shard_map.88 = bf16[64,1024]{1,0:T(8,128)(2,1)} custom-call(bf16[528,128]{1,0:T(8,128)(2,1)S(1)} %bitcast.7, bf16[528,128]{1,0:T(8,128)(2,1)S(1)} %collective-permute-done.9.refs_1_, bf16[528,128]{1,0:T(8,128)(2,1)S(1)} %collective-permute-done.10.refs_2_, bf16[528,128]{1,0:T(8,128)(2,1)S(1)} %collective-permute-done.11.refs_3_), custom_call_target="tpu_custom_call" | custom-call | tf_op jit(solution)/shard_map/pallas_call | solution.py:319
  (6 shorter events, 0.1 us)
Async XLA Ops:
  0.0 1.0 %slice-start = ((bf16[2048,128]{1,0:T(8,128)(2,1)}), bf16[1536,128]{1,0:T(8,128)(2,1)S(1)}, s32[]{:S(2)}) async-start(bf16[2048,128]{1,0:T(8,128)(2,1)} %param.11), calls=%async_computation | async-start | bytes 786432 | tf_op jit(solution)/shard_map/slice | solution.py:347
  0.0 1.1 %slice-start.2 = ((bf16[2048,128]{1,0:T(8,128)(2,1)}), bf16[1536,128]{1,0:T(8,128)(2,1)S(1)}, s32[]{:S(2)}) async-start(bf16[2048,128]{1,0:T(8,128)(2,1)} %param.12), calls=%async_computation.2 | async-start | bytes 786432 | tf_op jit(solution)/shard_map/slice | solution.py:347
  0.0 2.8 %slice-start.1 = ((bf16[2048,128]{1,0:T(8,128)(2,1)}), bf16[512,128]{1,0:T(8,128)(2,1)S(1)}, s32[]{:S(2)}) async-start(bf16[2048,128]{1,0:T(8,128)(2,1)} %param.11), calls=%async_computation.1 | async-start | bytes 262144 | tf_op jit(solution)/shard_map/slice | solution.py:349
  0.0 2.8 %slice-start.3 = ((bf16[2048,128]{1,0:T(8,128)(2,1)}), bf16[512,128]{1,0:T(8,128)(2,1)S(1)}, s32[]{:S(2)}) async-start(bf16[2048,128]{1,0:T(8,128)(2,1)} %param.12), calls=%async_computation.3 | async-start | bytes 262144 | tf_op jit(solution)/shard_map/slice | solution.py:349
  0.0 2.8 %copy-start.4 = (bf16[64,128]{1,0:T(8,128)(2,1)S(1)}, bf16[64,128]{1,0:T(8,128)(2,1)}, u32[]{:S(2)}) copy-start(bf16[64,128]{1,0:T(8,128)(2,1)} %param.10) | copy-start | bytes 49156
  0.0 2.8 %copy-start.5 = (bf16[64,128]{1,0:T(8,128)(2,1)S(1)}, bf16[64,128]{1,0:T(8,128)(2,1)}, u32[]{:S(2)}) copy-start(bf16[64,128]{1,0:T(8,128)(2,1)} %param.9) | copy-start | bytes 49156
  0.0 3.1 %copy-start.3 = (bf16[64,1024]{1,0:T(8,128)(2,1)S(1)}, bf16[64,1024]{1,0:T(8,128)(2,1)}, u32[]{:S(2)}) copy-start(bf16[64,1024]{1,0:T(8,128)(2,1)} %refs_3_.3) | copy-start | bytes 393220
  0.1 8.4 %copy-start = (s32[8]{0:T(128)S(1)}, s32[8]{0:T(128)}, u32[]{:S(2)}) copy-start(s32[8]{0:T(128)} %refs_0_.11) | copy-start | bytes 100
  0.1 8.4 %copy-start.1 = (s32[8]{0:T(128)S(1)}, s32[8]{0:T(128)}, u32[]{:S(2)}) copy-start(s32[8]{0:T(128)} %refs_1_.11) | copy-start | bytes 100
  0.1 8.4 %copy-start.2 = (s32[8]{0:T(128)S(1)}, s32[8]{0:T(128)}, u32[]{:S(2)}) copy-start(s32[8]{0:T(128)} %refs_2_.11) | copy-start | bytes 100
  1.2 7.3 %collective-permute-start.4 = (bf16[3072,128]{1,0:T(8,128)(2,1)S(1)}, bf16[3072,128]{1,0:T(8,128)(2,1)S(1)}, u32[]{:S(2)}, u32[]{:S(2)}) collective-permute-start(bf16[3072,128]{1,0:T(8,128)(2,1)S(1)} %pad_maximum_fusion.refs_4_.refs_5_), channel_id=1, source_target_pairs={{0,8},{8,0},{16,24},{24,16},{32,40},{40,32},{48,56},{56,48},{64,72... | collective-permute-start | bytes 2359304 | tf_op jit(solution)/shard_map/ppermute | solution.py:344
  1.3 22.3 %collective-permute-start = (bf16[3072,128]{1,0:T(8,128)(2,1)S(1)}, bf16[3072,128]{1,0:T(8,128)(2,1)S(1)}, u32[]{:S(2)}, u32[]{:S(2)}) collective-permute-start(bf16[3072,128]{1,0:T(8,128)(2,1)S(1)} %pad_maximum_fusion.refs_4_.refs_5_), channel_id=1, source_target_pairs={{0,64},{8,72},{16,80},{24,88},{32,96},{40,104},{48,112},{56,120},{... | collective-permute-start | bytes 2359304 | tf_op jit(solution)/shard_map/ppermute | solution.py:344
  2.9 4.3 %collective-permute-start.5 = (bf16[1152,128]{1,0:T(8,128)(2,1)S(1)}, bf16[1152,128]{1,0:T(8,128)(2,1)S(1)}, u32[]{:S(2)}, u32[]{:S(2)}) collective-permute-start(bf16[1152,128]{1,0:T(8,128)(2,1)S(1)} %pad_maximum_fusion.1.refs_5_.refs_6_), channel_id=1, source_target_pairs={{0,8},{8,0},{16,24},{24,16},{32,40},{40,32},{48,56},{56,48},{64,72... | collective-permute-start | bytes 884744 | tf_op jit(solution)/shard_map/ppermute | solution.py:344
  3.1 10.1 %collective-permute-start.3 = (bf16[64,1024]{1,0:T(8,128)(2,1)S(1)}, bf16[64,1024]{1,0:T(8,128)(2,1)S(1)}, u32[]{:S(2)}, u32[]{:S(2)}) collective-permute-start(bf16[64,1024]{1,0:T(8,128)(2,1)S(1)} %copy-done.3), channel_id=1, source_target_pairs={{0,48},{8,56},{16,0},{24,8},{32,16},{40,24},{48,32},{56,40},{64,11... | collective-permute-start | bytes 393224 | tf_op jit(solution)/shard_map/ppermute | solution.py:344
  7.2 9.7 %collective-permute-start.2 = (bf16[64,1024]{1,0:T(8,128)(2,1)S(1)}, bf16[64,1024]{1,0:T(8,128)(2,1)S(1)}, u32[]{:S(2)}, u32[]{:S(2)}) collective-permute-start(bf16[64,1024]{1,0:T(8,128)(2,1)S(1)} %copy-done.3), channel_id=1, source_target_pairs={{0,32},{8,40},{16,48},{24,56},{32,0},{40,8},{48,16},{56,24},{64,96... | collective-permute-start | bytes 393224 | tf_op jit(solution)/shard_map/ppermute | solution.py:344
  7.2 9.7 %collective-permute-start.1 = (bf16[64,1024]{1,0:T(8,128)(2,1)S(1)}, bf16[64,1024]{1,0:T(8,128)(2,1)S(1)}, u32[]{:S(2)}, u32[]{:S(2)}) collective-permute-start(bf16[64,1024]{1,0:T(8,128)(2,1)S(1)} %copy-done.3), channel_id=1, source_target_pairs={{0,16},{8,24},{16,32},{24,40},{32,48},{40,56},{48,0},{56,8},{64,80... | collective-permute-start | bytes 393224 | tf_op jit(solution)/shard_map/ppermute | solution.py:344
  23.5 2.4 %collective-permute-start.6 = (bf16[3072,128]{1,0:T(8,128)(2,1)S(1)}, bf16[3072,128]{1,0:T(8,128)(2,1)S(1)}, u32[]{:S(2)}, u32[]{:S(2)}) collective-permute-start(bf16[3072,128]{1,0:T(8,128)(2,1)S(1)} %collective-permute-done.refs_6_.refs_4_), channel_id=1, source_target_pairs={{0,8},{8,0},{16,24},{24,16},{32,40},{40,32},{48,56},{56,48},{64,72... | collective-permute-start | bytes 2359304 | tf_op jit(solution)/shard_map/ppermute | solution.py:344
  23.6 9.4 %collective-permute-start.7 = (bf16[1152,128]{1,0:T(8,128)(2,1)S(1)}, bf16[1152,128]{1,0:T(8,128)(2,1)S(1)}, u32[]{:S(2)}, u32[]{:S(2)}) collective-permute-start(bf16[1152,128]{1,0:T(8,128)(2,1)S(1)} %pad_maximum_fusion.1.refs_5_.refs_6_), channel_id=1, source_target_pairs={{0,64},{8,72},{16,80},{24,88},{32,96},{40,104},{48,112},{56,120},{... | collective-permute-start | bytes 884744 | tf_op jit(solution)/shard_map/ppermute | solution.py:344
  33.0 1.6 %collective-permute-start.8 = (bf16[1152,128]{1,0:T(8,128)(2,1)S(1)}, bf16[1152,128]{1,0:T(8,128)(2,1)S(1)}, u32[]{:S(2)}, u32[]{:S(2)}) collective-permute-start(bf16[1152,128]{1,0:T(8,128)(2,1)S(1)} %collective-permute-done.7.refs_6_), channel_id=1, source_target_pairs={{0,8},{8,0},{16,24},{24,16},{32,40},{40,32},{48,56},{56,48},{64,72... | collective-permute-start | bytes 884744 | tf_op jit(solution)/shard_map/ppermute | solution.py:344
  39.0 7.9 %collective-permute-start.11 = (bf16[528,128]{1,0:T(8,128)(2,1)S(1)}, bf16[528,128]{1,0:T(8,128)(2,1)S(1)}, u32[]{:S(2)}, u32[]{:S(2)}) collective-permute-start(bf16[528,128]{1,0:T(8,128)(2,1)S(1)} %get-tuple-element.23), channel_id=1, source_target_pairs={{0,32},{8,40},{16,48},{24,56},{32,0},{40,8},{48,16},{56,24},{64,96... | collective-permute-start | bytes 405512 | tf_op jit(solution)/shard_map/ppermute | solution.py:344
  40.6 9.6 %collective-permute-start.10 = (bf16[528,128]{1,0:T(8,128)(2,1)S(1)}, bf16[528,128]{1,0:T(8,128)(2,1)S(1)}, u32[]{:S(2)}, u32[]{:S(2)}) collective-permute-start(bf16[528,128]{1,0:T(8,128)(2,1)S(1)} %get-tuple-element.24), channel_id=1, source_target_pairs={{0,48},{8,56},{16,0},{24,8},{32,16},{40,24},{48,32},{56,40},{64,11... | collective-permute-start | bytes 405512 | tf_op jit(solution)/shard_map/ppermute | solution.py:344
  42.9 7.3 %collective-permute-start.9 = (bf16[528,128]{1,0:T(8,128)(2,1)S(1)}, bf16[528,128]{1,0:T(8,128)(2,1)S(1)}, u32[]{:S(2)}, u32[]{:S(2)}) collective-permute-start(bf16[528,128]{1,0:T(8,128)(2,1)S(1)} %get-tuple-element.25), channel_id=1, source_target_pairs={{0,16},{8,24},{16,32},{24,40},{32,48},{40,56},{48,0},{56,8},{64,80... | collective-permute-start | bytes 405512 | tf_op jit(solution)/shard_map/ppermute | solution.py:344

commit v2 on v1

--- a/solution.py
+++ b/solution.py
@@ -17,7 +17,7 @@
 SAMPLE = 256
 CUT = 1536
 SEGMENT = 512
-UNROLL = False
+UNROLL = True
 VMEM_LIMIT = 32 * 2**20
 NT = (((1,), (1,)), ((), ()))
 F32 = jnp.float32
@@ -196,7 +196,7 @@
     def quick():
         if len(state_in) > 1:
             restore()
-        if n == 1 or UNROLL:
+        if n < 3 or (emit and UNROLL):
             fixed_stabiliser(list(range(n)))
         else:
 
@@ -349,7 +349,7 @@
         [cache_keys[cut:], stretch_keys, cache_values[cut:], stretch_values], 0
     )
     messages = [(head_part, cut, 0, 0), (tail_part, shard - cut, own, cut)]
-    far = [send(message[0], flip_perm(count, 8)) for message in messages]
+    far0 = send(messages[0][0], flip_perm(count, 8))
     steps = [0, 3, 1, 2]
     chunks = [queries] + [send(queries, step_perm(count, s)) for s in steps[1:]]
     sibling = [send(message[0], flip_perm(count, 1)) for message in messages]
@@ -366,15 +366,17 @@
     near += [source(sibling[i], 1, i) for i in (0, 1)]
     others = [1, 2, 3]
     mine = call([0], near, [], False)
+    mine, later = lax.optimization_barrier((mine, messages[1][0]))
+    far1 = send(later, flip_perm(count, 8))
     chunks[1], mine = lax.optimization_barrier((chunks[1], mine))
     left = call([1], near, [], False)
     chunks[2], chunks[3], left = lax.optimization_barrier((*chunks[2:], left))
     right = call([2, 3], near, [], False)
-    far0, right = lax.optimization_barrier((far[0], right))
+    far0, right = lax.optimization_barrier((far0, right))
     far0_sibling = send(far0, flip_perm(count, 1))
     first = [source(far0, 8, 0), source(far0_sibling, 9, 0)]
     rest = call(others, first, [left, right], False)
-    far1, rest = lax.optimization_barrier((far[1], rest))
+    far1, rest = lax.optimization_barrier((far1, rest))
     far1_sibling = send(far1, flip_perm(count, 1))
     second = [source(far1, 8, 1), source(far1_sibling, 9, 1)]
     parts = call(others, second, [rest], True)

time: 51.5 us -> 50.3 us (0.977)
  Pallas kernels: 29.3 us -> 28 us
    pallas_call x6, Pallas kernels: 28.3 us -> 27 us  [attend(): pl.pallas_call(functools.partial(attend_kernel, geom), out_shape=out_shap...]
where the time goes in v2:
time: 50.3 us; the launch traced here: 50 us
  Pallas kernels  28 us (56%)
  starting transfers between devices  12.8 us (25%)
  waiting for transfers between devices  7.9 us (16%)
  local copies, waits for them, and re-layouts  1.1 us (2%)
    pallas_call x6, Pallas kernels, attend(): pl.pallas_call(functools.partial(attend_kernel, geom), out_shape=out_shap...  27 us
    ppermute x12, starting transfers between devices, send(): return lax.ppermute(x, 'ctx', perm)  12.8 us
    ppermute x12, waiting for transfers between devices, send(): return lax.ppermute(x, 'ctx', perm)  7.9 us
    slice x4, local copies, waits for them, and re-layouts, local(): head_part = jnp.concatenate([cache_keys[:cut], cache_values[:cut]], 0)  1.04 us
    pallas_call x1, Pallas kernels, combine(): pl.pallas_call(combine_kernel, out_shape=jax.ShapeDtypeStruct((tokens, wi...  1.02 us
  transfers between devices with their start and end apart: 12, of which 5 were waited for; matrix products, arithmetic and copies ran while one was open for 0% of the time, Pallas kernels for 47%

profile of v2, /device:TPU:16, one launch (start us, length us, event | category | flops | bytes accessed | tf_op | source)
XLA Modules:
  0.0 50.0 jit_solution(2269411754591459142)
XLA Ops:
  0.0 0.0 slice-start.3
  0.0 0.0 copy-start.4
  0.0 0.0 copy-start.5
  0.0 0.0 copy-start.3
  0.1 0.0 copy-start
  0.1 0.0 copy-start.1
  0.1 0.0 copy-start.2
  0.1 0.9 %slice-done = bf16[1536,128]{1,0:T(8,128)(2,1)S(1)} async-done(((bf16[2048,128]{1,0:T(8,128)(2,1)}), bf16[1536,128]{1,0:T(8,128)(2,1)S(1)}, s32[]{:S(2)}) %slice-start) | async-done | bytes 393240 | tf_op jit(solution)/shard_map/slice | solution.py:347
  1.0 0.1 slice-done.2
  1.1 0.1 pad_maximum_fusion.refs_4_.refs_5_
  1.2 0.1 collective-permute-start.4
  1.3 1.6 %collective-permute-start = (bf16[3072,128]{1,0:T(8,128)(2,1)S(1)}, bf16[3072,128]{1,0:T(8,128)(2,1)S(1)}, u32[]{:S(2)}, u32[]{:S(2)}) collective-permute-start(bf16[3072,128]{1,0:T(8,128)(2,1)S(1)} %pad_maximum_fusion.refs_4_.refs_5_), channel_id=1, source_target_pairs={{0,64},{8,72},{16,80},{24,88},{32,96},{40,104},{48,112},{56,120},{... | collective-permute-start | bytes 2359304 | tf_op jit(solution)/shard_map/ppermute | solution.py:344
  2.8 0.0 slice-done.1
  2.8 0.0 slice-done.3
  2.8 0.0 copy-done.4
  2.8 0.0 copy-done.5
  2.9 0.2 collective-permute-start.5
  3.1 0.0 copy-done.3
  3.1 4.1 %collective-permute-start.3 = (bf16[64,1024]{1,0:T(8,128)(2,1)S(1)}, bf16[64,1024]{1,0:T(8,128)(2,1)S(1)}, u32[]{:S(2)}, u32[]{:S(2)}) collective-permute-start(bf16[64,1024]{1,0:T(8,128)(2,1)S(1)} %copy-done.3), channel_id=1, source_target_pairs={{0,48},{8,56},{16,0},{24,8},{32,16},{40,24},{48,32},{56,40},{64,11... | collective-permute-start | bytes 393224 | tf_op jit(solution)/shard_map/ppermute | solution.py:344
  7.2 0.0 collective-permute-start.2
  7.2 0.0 collective-permute-done.5.refs_7_.refs_8_
  7.2 1.3 %collective-permute-start.1 = (bf16[64,1024]{1,0:T(8,128)(2,1)S(1)}, bf16[64,1024]{1,0:T(8,128)(2,1)S(1)}, u32[]{:S(2)}, u32[]{:S(2)}) collective-permute-start(bf16[64,1024]{1,0:T(8,128)(2,1)S(1)} %copy-done.3), channel_id=1, source_target_pairs={{0,16},{8,24},{16,32},{24,40},{32,48},{40,56},{48,0},{56,8},{64,80... | collective-permute-start | bytes 393224 | tf_op jit(solution)/shard_map/ppermute | solution.py:344
  8.4 0.0 collective-permute-done.4.refs_6_.refs_7_
  8.4 0.0 copy-done.1
  8.4 0.0 copy-done.2
  8.4 3.4 %shard_map.82.refs_8_ = f32[1,3,512,128]{3,2,1,0:T(8,128)S(1)} custom-call(s32[8]{0:T(128)S(1)} %copy-done, s32[8]{0:T(128)S(1)} %copy-done.1, s32[8]{0:T(128)S(1)} %copy-done.2, bf16[64,1024]{1,0:T(8,128)(2,1)S(1)} %copy-done.3, bf16[3072,128]{1,0:T(8,128)(2,1)S(1)} %pad_maximum_fusion.refs_4_.refs_5_, ...), custom_call_target="tpu_custom_call" | custom-call | flops 1107296256 | bytes 2162688 | tf_op jit(solution)/shard_map/pallas_call | solution.py:278
  11.9 1.4 %collective-permute-done.3.refs_3_ = bf16[64,1024]{1,0:T(8,128)(2,1)S(1)} collective-permute-done((bf16[64,1024]{1,0:T(8,128)(2,1)S(1)}, bf16[64,1024]{1,0:T(8,128)(2,1)S(1)}, u32[]{:S(2)}, u32[]{:S(2)}) %collective-permute-start.3) | collective-permute-done | bytes 131104 | tf_op jit(solution)/shard_map/ppermute | solution.py:344
  13.2 3.6 %shard_map.83.refs_8_ = f32[1,3,512,128]{3,2,1,0:T(8,128)S(1)} custom-call(s32[8]{0:T(128)S(1)} %copy-done, s32[8]{0:T(128)S(1)} %copy-done.1, s32[8]{0:T(128)S(1)} %copy-done.2, bf16[64,1024]{1,0:T(8,128)(2,1)S(1)} %collective-permute-done.3.refs_3_, bf16[3072,128]{1,0:T(8,128)(2,1)S(1)} %pad_maximum_fusion.refs_4_.refs_5_, ...), custom_call_target="tpu_custom_call" | custom-call | flops 1107296256 | bytes 2162688 | tf_op jit(solution)/shard_map/pallas_call | solution.py:278
  16.9 0.0 collective-permute-done.2.refs_4_.refs_5_
  16.9 0.0 collective-permute-done.1.refs_3_.refs_4_
  16.9 6.0 %shard_map.84.refs_9_ = f32[2,3,512,128]{3,2,1,0:T(8,128)S(1)} custom-call(s32[8]{0:T(128)S(1)} %copy-done, s32[8]{0:T(128)S(1)} %copy-done.1, s32[8]{0:T(128)S(1)} %copy-done.2, bf16[64,1024]{1,0:T(8,128)(2,1)S(1)} %collective-permute-done.1.refs_3_.refs_4_, bf16[64,1024]{1,0:T(8,128)(2,1)S(1)} %collective-permute-done.2.refs_4_.refs_5_, ...), custom_call_target="tpu_custom_call" | custom-call | flops 2214592512 | bytes 2162688 | tf_op jit(solution)/shard_map/pallas_call | solution.py:278
  22.9 0.0 collective-permute-done.refs_6_.refs_4_
  22.9 0.1 collective-permute-start.6
  23.0 0.6 %collective-permute-start.7 = (bf16[1152,128]{1,0:T(8,128)(2,1)S(1)}, bf16[1152,128]{1,0:T(8,128)(2,1)S(1)}, u32[]{:S(2)}, u32[]{:S(2)}) collective-permute-start(bf16[1152,128]{1,0:T(8,128)(2,1)S(1)} %pad_maximum_fusion.1.refs_5_.refs_6_), channel_id=1, source_target_pairs={{0,64},{8,72},{16,80},{24,88},{32,96},{40,104},{48,112},{56,120},{... | collective-permute-start | bytes 884744 | tf_op jit(solution)/shard_map/ppermute | solution.py:344
  23.6 1.7 %collective-permute-done.6.refs_7_.refs_5_ = bf16[3072,128]{1,0:T(8,128)(2,1)S(1)} collective-permute-done((bf16[3072,128]{1,0:T(8,128)(2,1)S(1)}, bf16[3072,128]{1,0:T(8,128)(2,1)S(1)}, u32[]{:S(2)}, u32[]{:S(2)}) %collective-permute-start.6) | collective-permute-done | bytes 786464 | tf_op jit(solution)/shard_map/ppermute | solution.py:344
  25.3 7.0 %shard_map.85.refs_8_ = f32[3,3,512,128]{3,2,1,0:T(8,128)S(1)} custom-call(s32[8]{0:T(128)S(1)} %copy-done, s32[8]{0:T(128)S(1)} %copy-done.1, s32[8]{0:T(128)S(1)} %copy-done.2, bf16[64,1024]{1,0:T(8,128)(2,1)S(1)} %collective-permute-done.3.refs_3_, bf16[64,1024]{1,0:T(8,128)(2,1)S(1)} %collective-permute-done.1.refs_3_.refs_4_, ...), custom_call_target="tpu_custom_call" | custom-call | flops 2415919104 | bytes 1572864 | tf_op jit(solution)/shard_map/pallas_call | solution.py:278
  32.3 0.2 collective-permute-done.7.refs_6_
  32.5 0.3 collective-permute-start.8
  32.7 1.4 %collective-permute-done.8.refs_7_ = bf16[1152,128]{1,0:T(8,128)(2,1)S(1)} collective-permute-done((bf16[1152,128]{1,0:T(8,128)(2,1)S(1)}, bf16[1152,128]{1,0:T(8,128)(2,1)S(1)}, u32[]{:S(2)}, u32[]{:S(2)}) %collective-permute-start.8) | collective-permute-done | bytes 294944 | tf_op jit(solution)/shard_map/ppermute | solution.py:344
  34.2 3.6 %shard_map.87 = bf16[3,528,128]{2,1,0:T(8,128)(2,1)S(1)} custom-call(s32[8]{0:T(128)S(1)} %copy-done, s32[8]{0:T(128)S(1)} %copy-done.1, s32[8]{0:T(128)S(1)} %copy-done.2, bf16[64,1024]{1,0:T(8,128)(2,1)S(1)} %collective-permute-done.3.refs_3_, bf16[64,1024]{1,0:T(8,128)(2,1)S(1)} %collective-permute-done.1.refs_3_.refs_4_, ...), custom_call_target="tpu_custom_call" | custom-call | flops 905969664 | bytes 589824 | tf_op jit(solution)/shard_map/pallas_call | solution.py:278
  37.8 2.2 %collective-permute-start.11 = (bf16[528,128]{1,0:T(8,128)(2,1)S(1)}, bf16[528,128]{1,0:T(8,128)(2,1)S(1)}, u32[]{:S(2)}, u32[]{:S(2)}) collective-permute-start(bf16[528,128]{1,0:T(8,128)(2,1)S(1)} %get-tuple-element.27), channel_id=1, source_target_pairs={{0,32},{8,40},{16,48},{24,56},{32,0},{40,8},{48,16},{56,24},{64,96... | collective-permute-start | bytes 405512 | tf_op jit(solution)/shard_map/ppermute | solution.py:344
  40.0 1.7 %collective-permute-start.10 = (bf16[528,128]{1,0:T(8,128)(2,1)S(1)}, bf16[528,128]{1,0:T(8,128)(2,1)S(1)}, u32[]{:S(2)}, u32[]{:S(2)}) collective-permute-start(bf16[528,128]{1,0:T(8,128)(2,1)S(1)} %get-tuple-element.28), channel_id=1, source_target_pairs={{0,48},{8,56},{16,0},{24,8},{32,16},{40,24},{48,32},{56,40},{64,11... | collective-permute-start | bytes 405512 | tf_op jit(solution)/shard_map/ppermute | solution.py:344
  41.7 0.8 %collective-permute-start.9 = (bf16[528,128]{1,0:T(8,128)(2,1)S(1)}, bf16[528,128]{1,0:T(8,128)(2,1)S(1)}, u32[]{:S(2)}, u32[]{:S(2)}) collective-permute-start(bf16[528,128]{1,0:T(8,128)(2,1)S(1)} %get-tuple-element.29), channel_id=1, source_target_pairs={{0,16},{8,24},{16,32},{24,40},{32,48},{40,56},{48,0},{56,8},{64,80... | collective-permute-start | bytes 405512 | tf_op jit(solution)/shard_map/ppermute | solution.py:344
  42.5 3.3 %shard_map.86 = bf16[1,528,128]{2,1,0:T(8,128)(2,1)S(1)} custom-call(s32[8]{0:T(128)S(1)} %copy-done, s32[8]{0:T(128)S(1)} %copy-done.1, s32[8]{0:T(128)S(1)} %copy-done.2, bf16[64,1024]{1,0:T(8,128)(2,1)S(1)} %copy-done.3, bf16[3072,128]{1,0:T(8,128)(2,1)S(1)} %collective-permute-done.refs_6_.refs_4_, ...), custom_call_target="tpu_custom_call" | custom-call | flops 1107296256 | bytes 2162688 | tf_op jit(solution)/shard_map/pallas_call | solution.py:278
  45.8 0.0 collective-permute-done.11.refs_3_
  45.8 3.2 %collective-permute-done.10.refs_2_ = bf16[528,128]{1,0:T(8,128)(2,1)S(1)} collective-permute-done((bf16[528,128]{1,0:T(8,128)(2,1)S(1)}, bf16[528,128]{1,0:T(8,128)(2,1)S(1)}, u32[]{:S(2)}, u32[]{:S(2)}) %collective-permute-start.10) | collective-permute-done | bytes 135200 | tf_op jit(solution)/shard_map/ppermute | solution.py:344
  49.0 0.0 collective-permute-done.9.refs_1_
  49.0 1.0 %shard_map.88 = bf16[64,1024]{1,0:T(8,128)(2,1)} custom-call(bf16[528,128]{1,0:T(8,128)(2,1)S(1)} %bitcast.7, bf16[528,128]{1,0:T(8,128)(2,1)S(1)} %collective-permute-done.9.refs_1_, bf16[528,128]{1,0:T(8,128)(2,1)S(1)} %collective-permute-done.10.refs_2_, bf16[528,128]{1,0:T(8,128)(2,1)S(1)} %collective-permute-done.11.refs_3_), custom_call_target="tpu_custom_call" | custom-call | tf_op jit(solution)/shard_map/pallas_call | solution.py:319
  (6 shorter events, 0.1 us)
Async XLA Ops:
  0.0 1.0 %slice-start = ((bf16[2048,128]{1,0:T(8,128)(2,1)}), bf16[1536,128]{1,0:T(8,128)(2,1)S(1)}, s32[]{:S(2)}) async-start(bf16[2048,128]{1,0:T(8,128)(2,1)} %param.11), calls=%async_computation | async-start | bytes 786432 | tf_op jit(solution)/shard_map/slice | solution.py:347
  0.0 1.1 %slice-start.2 = ((bf16[2048,128]{1,0:T(8,128)(2,1)}), bf16[1536,128]{1,0:T(8,128)(2,1)S(1)}, s32[]{:S(2)}) async-start(bf16[2048,128]{1,0:T(8,128)(2,1)} %param.12), calls=%async_computation.2 | async-start | bytes 786432 | tf_op jit(solution)/shard_map/slice | solution.py:347
  0.0 2.8 %slice-start.1 = ((bf16[2048,128]{1,0:T(8,128)(2,1)}), bf16[512,128]{1,0:T(8,128)(2,1)S(1)}, s32[]{:S(2)}) async-start(bf16[2048,128]{1,0:T(8,128)(2,1)} %param.11), calls=%async_computation.1 | async-start | bytes 262144 | tf_op jit(solution)/shard_map/slice | solution.py:349
  0.0 2.8 %slice-start.3 = ((bf16[2048,128]{1,0:T(8,128)(2,1)}), bf16[512,128]{1,0:T(8,128)(2,1)S(1)}, s32[]{:S(2)}) async-start(bf16[2048,128]{1,0:T(8,128)(2,1)} %param.12), calls=%async_computation.3 | async-start | bytes 262144 | tf_op jit(solution)/shard_map/slice | solution.py:349
  0.0 2.8 %copy-start.4 = (bf16[64,128]{1,0:T(8,128)(2,1)S(1)}, bf16[64,128]{1,0:T(8,128)(2,1)}, u32[]{:S(2)}) copy-start(bf16[64,128]{1,0:T(8,128)(2,1)} %param.10) | copy-start | bytes 49156
  0.0 2.8 %copy-start.5 = (bf16[64,128]{1,0:T(8,128)(2,1)S(1)}, bf16[64,128]{1,0:T(8,128)(2,1)}, u32[]{:S(2)}) copy-start(bf16[64,128]{1,0:T(8,128)(2,1)} %param.9) | copy-start | bytes 49156
  0.0 3.1 %copy-start.3 = (bf16[64,1024]{1,0:T(8,128)(2,1)S(1)}, bf16[64,1024]{1,0:T(8,128)(2,1)}, u32[]{:S(2)}) copy-start(bf16[64,1024]{1,0:T(8,128)(2,1)} %refs_3_.3) | copy-start | bytes 393220
  0.1 8.4 %copy-start = (s32[8]{0:T(128)S(1)}, s32[8]{0:T(128)}, u32[]{:S(2)}) copy-start(s32[8]{0:T(128)} %refs_0_.11) | copy-start | bytes 100
  0.1 8.4 %copy-start.1 = (s32[8]{0:T(128)S(1)}, s32[8]{0:T(128)}, u32[]{:S(2)}) copy-start(s32[8]{0:T(128)} %refs_1_.11) | copy-start | bytes 100
  0.1 8.4 %copy-start.2 = (s32[8]{0:T(128)S(1)}, s32[8]{0:T(128)}, u32[]{:S(2)}) copy-start(s32[8]{0:T(128)} %refs_2_.11) | copy-start | bytes 100
  1.2 7.3 %collective-permute-start.4 = (bf16[3072,128]{1,0:T(8,128)(2,1)S(1)}, bf16[3072,128]{1,0:T(8,128)(2,1)S(1)}, u32[]{:S(2)}, u32[]{:S(2)}) collective-permute-start(bf16[3072,128]{1,0:T(8,128)(2,1)S(1)} %pad_maximum_fusion.refs_4_.refs_5_), channel_id=1, source_target_pairs={{0,8},{8,0},{16,24},{24,16},{32,40},{40,32},{48,56},{56,48},{64,72... | collective-permute-start | bytes 2359304 | tf_op jit(solution)/shard_map/ppermute | solution.py:344
  1.3 21.7 %collective-permute-start = (bf16[3072,128]{1,0:T(8,128)(2,1)S(1)}, bf16[3072,128]{1,0:T(8,128)(2,1)S(1)}, u32[]{:S(2)}, u32[]{:S(2)}) collective-permute-start(bf16[3072,128]{1,0:T(8,128)(2,1)S(1)} %pad_maximum_fusion.refs_4_.refs_5_), channel_id=1, source_target_pairs={{0,64},{8,72},{16,80},{24,88},{32,96},{40,104},{48,112},{56,120},{... | collective-permute-start | bytes 2359304 | tf_op jit(solution)/shard_map/ppermute | solution.py:344
  2.9 4.3 %collective-permute-start.5 = (bf16[1152,128]{1,0:T(8,128)(2,1)S(1)}, bf16[1152,128]{1,0:T(8,128)(2,1)S(1)}, u32[]{:S(2)}, u32[]{:S(2)}) collective-permute-start(bf16[1152,128]{1,0:T(8,128)(2,1)S(1)} %pad_maximum_fusion.1.refs_5_.refs_6_), channel_id=1, source_target_pairs={{0,8},{8,0},{16,24},{24,16},{32,40},{40,32},{48,56},{56,48},{64,72... | collective-permute-start | bytes 884744 | tf_op jit(solution)/shard_map/ppermute | solution.py:344
  3.1 10.1 %collective-permute-start.3 = (bf16[64,1024]{1,0:T(8,128)(2,1)S(1)}, bf16[64,1024]{1,0:T(8,128)(2,1)S(1)}, u32[]{:S(2)}, u32[]{:S(2)}) collective-permute-start(bf16[64,1024]{1,0:T(8,128)(2,1)S(1)} %copy-done.3), channel_id=1, source_target_pairs={{0,48},{8,56},{16,0},{24,8},{32,16},{40,24},{48,32},{56,40},{64,11... | collective-permute-start | bytes 393224 | tf_op jit(solution)/shard_map/ppermute | solution.py:344
  7.2 9.7 %collective-permute-start.2 = (bf16[64,1024]{1,0:T(8,128)(2,1)S(1)}, bf16[64,1024]{1,0:T(8,128)(2,1)S(1)}, u32[]{:S(2)}, u32[]{:S(2)}) collective-permute-start(bf16[64,1024]{1,0:T(8,128)(2,1)S(1)} %copy-done.3), channel_id=1, source_target_pairs={{0,32},{8,40},{16,48},{24,56},{32,0},{40,8},{48,16},{56,24},{64,96... | collective-permute-start | bytes 393224 | tf_op jit(solution)/shard_map/ppermute | solution.py:344
  7.2 9.7 %collective-permute-start.1 = (bf16[64,1024]{1,0:T(8,128)(2,1)S(1)}, bf16[64,1024]{1,0:T(8,128)(2,1)S(1)}, u32[]{:S(2)}, u32[]{:S(2)}) collective-permute-start(bf16[64,1024]{1,0:T(8,128)(2,1)S(1)} %copy-done.3), channel_id=1, source_target_pairs={{0,16},{8,24},{16,32},{24,40},{32,48},{40,56},{48,0},{56,8},{64,80... | collective-permute-start | bytes 393224 | tf_op jit(solution)/shard_map/ppermute | solution.py:344
  22.9 2.4 %collective-permute-start.6 = (bf16[3072,128]{1,0:T(8,128)(2,1)S(1)}, bf16[3072,128]{1,0:T(8,128)(2,1)S(1)}, u32[]{:S(2)}, u32[]{:S(2)}) collective-permute-start(bf16[3072,128]{1,0:T(8,128)(2,1)S(1)} %collective-permute-done.refs_6_.refs_4_), channel_id=1, source_target_pairs={{0,8},{8,0},{16,24},{24,16},{32,40},{40,32},{48,56},{56,48},{64,72... | collective-permute-start | bytes 2359304 | tf_op jit(solution)/shard_map/ppermute | solution.py:344
  23.0 9.4 %collective-permute-start.7 = (bf16[1152,128]{1,0:T(8,128)(2,1)S(1)}, bf16[1152,128]{1,0:T(8,128)(2,1)S(1)}, u32[]{:S(2)}, u32[]{:S(2)}) collective-permute-start(bf16[1152,128]{1,0:T(8,128)(2,1)S(1)} %pad_maximum_fusion.1.refs_5_.refs_6_), channel_id=1, source_target_pairs={{0,64},{8,72},{16,80},{24,88},{32,96},{40,104},{48,112},{56,120},{... | collective-permute-start | bytes 884744 | tf_op jit(solution)/shard_map/ppermute | solution.py:344
  32.5 1.7 %collective-permute-start.8 = (bf16[1152,128]{1,0:T(8,128)(2,1)S(1)}, bf16[1152,128]{1,0:T(8,128)(2,1)S(1)}, u32[]{:S(2)}, u32[]{:S(2)}) collective-permute-start(bf16[1152,128]{1,0:T(8,128)(2,1)S(1)} %collective-permute-done.7.refs_6_), channel_id=1, source_target_pairs={{0,8},{8,0},{16,24},{24,16},{32,40},{40,32},{48,56},{56,48},{64,72... | collective-permute-start | bytes 884744 | tf_op jit(solution)/shard_map/ppermute | solution.py:344
  37.8 7.9 %collective-permute-start.11 = (bf16[528,128]{1,0:T(8,128)(2,1)S(1)}, bf16[528,128]{1,0:T(8,128)(2,1)S(1)}, u32[]{:S(2)}, u32[]{:S(2)}) collective-permute-start(bf16[528,128]{1,0:T(8,128)(2,1)S(1)} %get-tuple-element.27), channel_id=1, source_target_pairs={{0,32},{8,40},{16,48},{24,56},{32,0},{40,8},{48,16},{56,24},{64,96... | collective-permute-start | bytes 405512 | tf_op jit(solution)/shard_map/ppermute | solution.py:344
  40.0 9.0 %collective-permute-start.10 = (bf16[528,128]{1,0:T(8,128)(2,1)S(1)}, bf16[528,128]{1,0:T(8,128)(2,1)S(1)}, u32[]{:S(2)}, u32[]{:S(2)}) collective-permute-start(bf16[528,128]{1,0:T(8,128)(2,1)S(1)} %get-tuple-element.28), channel_id=1, source_target_pairs={{0,48},{8,56},{16,0},{24,8},{32,16},{40,24},{48,32},{56,40},{64,11... | collective-permute-start | bytes 405512 | tf_op jit(solution)/shard_map/ppermute | solution.py:344
  41.7 7.3 %collective-permute-start.9 = (bf16[528,128]{1,0:T(8,128)(2,1)S(1)}, bf16[528,128]{1,0:T(8,128)(2,1)S(1)}, u32[]{:S(2)}, u32[]{:S(2)}) collective-permute-start(bf16[528,128]{1,0:T(8,128)(2,1)S(1)} %get-tuple-element.29), channel_id=1, source_target_pairs={{0,16},{8,24},{16,32},{24,40},{32,48},{40,56},{48,0},{56,8},{64,80... | collective-permute-start | bytes 405512 | tf_op jit(solution)/shard_map/ppermute | solution.py:344
